TPU v7x, 32 devices: a whole 2x2x4 slice. The times are simulated.
32 devices in a mesh: groups: 2 (over x), rows: 8 (over z, y), shots: 2 (over core).
Axes of the slice: x: 2, y: 2, z: 4, core: 2. Of those that a mesh axis runs over, the one named last changes fastest.
Arguments:
- right_sides: bfloat16 [2, 16384, 512], P(None, 'rows', ('groups', 'shots')), parts along dimension 2, may hold values from -6 to 6
- panels: bfloat16 [2, 32768, 1024], P(None, ('groups', 'rows')), parts along dimension 1, may hold values from -0.125 to 0.125
- inverses: bfloat16 [8, 2, 256, 256], P('groups'), parts along dimension 0, may hold values from -0.25 to 0.25
- pivots: int32 [4], replicated, may hold values from 0 to 63, as said below
Outputs:
- regrouped: bfloat16 [2, 2, 256, 16384], P(None, 'shots', ('groups', 'rows')), parts along dimension 2
There are 2 independent parts, one for each index of `groups`. A program takes and returns all parts, laid end to end along the dimension named above; an argument that names none is the same for every part. Nothing has to cross between parts.
Inputs may be any that keep to these rules, and one draw needn't show every extreme that they name: `pivots`: 4 distinct row block numbers.
All inputs are finite; a program needn't handle non-finite values.
Results may differ from a plain program's by a relative error of at most 0.0052.
Values may be sent and summed in bfloat16 or wider, within the bound.
No kernel may reach another device: no remote copies, remote signals or barrier semaphores. Data moves between devices by JAX's collectives and lax.ppermute only.
A program may use at most 64 MiB of HBM per device.

v0:
```python
import functools

import jax
import jax.numpy as jnp
from jax import lax
from jax.experimental import pallas as pl
from jax.experimental.pallas import tpu as pltpu
from jax.sharding import PartitionSpec as P

CONTRACT_LAST = (((1,), (1,)), ((), ()))

BESIDE_PANELS = pltpu.CompilerParams(vmem_limit_bytes=57 * 1024 * 1024)
TILES = 4
SMALL = pltpu.CompilerParams(vmem_limit_bytes=16 * 1024 * 1024)


def dot_t(left, right):
    return lax.dot_general(left, right, CONTRACT_LAST, preferred_element_type=jnp.float32)


def turned(vectors):
    half = vectors.shape[0] // 2
    return jnp.concatenate([-vectors[half:], vectors[:half]], axis=0)


def transposed_sides(sides):
    shots = sides.shape[2]
    row = lax.broadcasted_iota(jnp.int32, (shots, shots), 0)
    column = lax.broadcasted_iota(jnp.int32, (shots, shots), 1)
    unit = jnp.where(row == column, 1.0, 0.0).astype(jnp.bfloat16)
    return jnp.concatenate([dot_t(unit, sides[0]), dot_t(unit, sides[1])], axis=0)


def first_kernel(per_device, pivots_ref, sides_ref, inverse_ref, out_ref, *owner_refs):
    for panel, owner_ref in enumerate(owner_refs):
        owner_ref[0] = lax.div(pivots_ref[panel], per_device)
    rows = transposed_sides(sides_ref).astype(jnp.bfloat16)
    solved = dot_t(rows, inverse_ref[0, 0]) + dot_t(turned(rows), inverse_ref[0, 1])
    out_ref[...] = solved.astype(jnp.bfloat16)


def solve_first(pivots, right_sides, inverses):
    parts, local_rows, shots = right_sides.shape
    count, width = inverses.shape[0], inverses.shape[-1]
    per_device = local_rows // width
    return pl.pallas_call(
        functools.partial(first_kernel, per_device),
        out_shape=[jax.ShapeDtypeStruct((parts * shots, width), jnp.bfloat16)]
        + [jax.ShapeDtypeStruct((1,), jnp.int32)] * count,
        grid_spec=pltpu.PrefetchScalarGridSpec(
            num_scalar_prefetch=1,
            grid=(1,),
            in_specs=[
                pl.BlockSpec((parts, width, shots), lambda i, p: (0, lax.rem(p[0], per_device), 0)),
                pl.BlockSpec((1, parts, width, width), lambda i, *_: (0, 0, 0, 0)),
            ],
            out_specs=[pl.BlockSpec((parts * shots, width), lambda i, *_: (0, 0))]
            + [pl.BlockSpec(memory_space=pltpu.SMEM)] * count,
        ),
        compiler_params=BESIDE_PANELS,
        name="solve_first",
    )(pivots, right_sides, inverses)


def prepare_kernel(count, pivots_ref, inverse_ref, *refs):
    sides_refs, panel_refs, out_refs = refs[: count - 1], refs[count - 1 : 2 * count - 2], refs[2 * count - 2 :]
    for panel, (sides_ref, panel_ref, out_ref) in enumerate(zip(sides_refs, panel_refs, out_refs), 1):
        parts, width, shots = sides_ref.shape
        for part in range(parts):
            out_ref[part * width : (part + 1) * width] = inverse_ref[panel, part]
        start = parts * width
        out_ref[start : start + parts * shots] = transposed_sides(sides_ref).astype(jnp.bfloat16)
        start += parts * shots
        pieces = [(j, p) for j in range(panel_ref.shape[2] // width) for p in range(parts)]
        for n, (j, p) in enumerate(pieces):
            out_ref[start + n * width : start + (n + 1) * width] = panel_ref[p, :, j * width : (j + 1) * width]


def prepare(pivots, right_sides, panels, inverses):
    parts, local_rows, shots = right_sides.shape
    count, width = inverses.shape[0], inverses.shape[-1]
    per_device = local_rows // width

    def slot(panel):
        return lambda i, pivots_ref: (0, lax.rem(pivots_ref[panel], per_device), 0)

    shapes = [(parts * (shots + (panel + 1) * width), width) for panel in range(1, count)]
    return pl.pallas_call(
        functools.partial(prepare_kernel, count),
        out_shape=[jax.ShapeDtypeStruct(shape, jnp.bfloat16) for shape in shapes],
        grid_spec=pltpu.PrefetchScalarGridSpec(
            num_scalar_prefetch=1,
            grid=(1,),
            in_specs=[pl.BlockSpec(inverses.shape, lambda i, *_: (0, 0, 0, 0))]
            + [pl.BlockSpec((parts, width, shots), slot(panel)) for panel in range(1, count)]
            + [pl.BlockSpec((parts, width, panel * width), slot(panel)) for panel in range(1, count)],
            out_specs=[pl.BlockSpec(shape, lambda i, *_: (0, 0)) for shape in shapes],
        ),
        compiler_params=BESIDE_PANELS,
        name="prepare",
    )(pivots, inverses, *[right_sides] * (count - 1), *[panels] * (count - 1))


def solve_kernel(own_ref, *refs):
    solved_refs, out_ref = refs[:-1], refs[-1]
    height, width = out_ref.shape
    start = 2 * width + height
    rows = own_ref[2 * width : start].astype(jnp.float32)
    for solved_ref in solved_refs:
        solved = solved_ref[...]
        rows = rows - dot_t(solved, own_ref[start : start + width])
        rows = rows - dot_t(turned(solved), own_ref[start + width : start + 2 * width])
        start += 2 * width
    rows = rows.astype(jnp.bfloat16)
    solved = dot_t(rows, own_ref[:width]) + dot_t(turned(rows), own_ref[width : 2 * width])
    out_ref[...] = solved.astype(jnp.bfloat16)


def solve(own, solved):
    height, width = solved[0].shape
    return pl.pallas_call(
        solve_kernel,
        out_shape=jax.ShapeDtypeStruct((height, width), jnp.bfloat16),
        grid=(1,),
        in_specs=[pl.BlockSpec(own.shape, lambda i: (0, 0))]
        + [pl.BlockSpec(block.shape, lambda i: (0, 0)) for block in solved],
        out_specs=pl.BlockSpec((height, width), lambda i: (0, 0)),
        compiler_params=SMALL,
        name="solve",
    )(own, *solved)


def early_kernel(sides_ref, panel_ref, *refs):
    solved_refs, (out_ref, real_ref, imag_ref) = refs[:-3], refs[-3:]
    width = solved_refs[0].shape[1]

    @pl.when(pl.program_id(0) == 0)
    def _():
        for j, solved_ref in enumerate(solved_refs):
            solved = solved_ref[...]
            real_ref[:, j * width : (j + 1) * width] = solved
            imag_ref[:, j * width : (j + 1) * width] = turned(solved)

    values = transposed_sides(sides_ref) - dot_t(real_ref[...], panel_ref[0])
    out_ref[...] = values - dot_t(imag_ref[...], panel_ref[1])


def early_update(right_sides, panels, solved):
    parts, local_rows, shots = right_sides.shape
    height, width = solved[0].shape
    columns = len(solved) * width
    tile = TILES * width if local_rows % (TILES * width) == 0 else width
    return pl.pallas_call(
        early_kernel,
        out_shape=jax.ShapeDtypeStruct((height, local_rows), jnp.float32),
        grid=(local_rows // tile,),
        in_specs=[
            pl.BlockSpec((parts, tile, shots), lambda i: (0, i, 0)),
            pl.BlockSpec((parts, tile, columns), lambda i: (0, i, 0)),
        ]
        + [pl.BlockSpec((height, width), lambda i: (0, 0)) for _ in solved],
        out_specs=pl.BlockSpec((height, tile), lambda i: (0, i)),
        scratch_shapes=[pltpu.VMEM((height, columns), jnp.bfloat16)] * 2,
        compiler_params=BESIDE_PANELS,
        name="early_update",
    )(right_sides, panels, *solved)


def last_kernel(owners, pivots_ref, first_ref, running_ref, panel_ref, *refs):
    solved_refs, out_ref = refs[:-1], refs[-1]
    rows = running_ref.shape[1]
    width = solved_refs[0].shape[1]
    solved = solved_refs[-1][...]
    values = running_ref[...] - dot_t(solved, panel_ref[0]) - dot_t(turned(solved), panel_ref[1])
    shots = values.shape[0] // 2
    each = shots // owners

    def write(block, columns):
        for part in range(2):
            for owner in range(owners):
                start = part * shots + owner * each
                out_ref[owner, part, :, columns] = block[start : start + each]

    write(values.astype(jnp.bfloat16), slice(None))
    first = first_ref[0] + pl.program_id(0) * (rows // width)
    for j, solved_ref in enumerate(solved_refs):
        for k in range(rows // width):

            @pl.when(pivots_ref[j] == first + k)
            def _():
                write(solved_ref[...], slice(k * width, (k + 1) * width))


def last_update(first, pivots, running, panels, solved, owners):
    parts, local_rows, columns = panels.shape
    height, width = solved[0].shape
    each = height // parts // owners
    tile = TILES * width if local_rows % (TILES * width) == 0 else width
    return pl.pallas_call(
        functools.partial(last_kernel, owners),
        out_shape=jax.ShapeDtypeStruct((owners, parts, each, local_rows), jnp.bfloat16),
        grid_spec=pltpu.PrefetchScalarGridSpec(
            num_scalar_prefetch=2,
            grid=(local_rows // tile,),
            in_specs=[
                pl.BlockSpec((height, tile), lambda i, *_: (0, i)),
                pl.BlockSpec((parts, tile, width), lambda i, *_: (0, i, columns // width - 1)),
            ]
            + [pl.BlockSpec(block.shape, lambda i, *_: (0, 0)) for block in solved],
            out_specs=pl.BlockSpec((owners, parts, each, tile), lambda i, *_: (0, 0, 0, i)),
        ),
        compiler_params=BESIDE_PANELS,
        name="last_update",
    )(pivots, first, running, panels, *solved)


def regroup_kernel(rows_ref, out_ref, sems):
    owners, _, _, rows = rows_ref.shape
    copies = [
        pltpu.make_async_copy(rows_ref.at[owner], out_ref.at[:, 0, :, pl.ds(owner * rows, rows)], sems.at[owner])
        for owner in range(owners)
    ]
    for copy in copies:
        copy.start()
    for copy in copies:
        copy.wait()


def regroup(received):
    owners, parts, shots, rows = received.shape
    return pl.pallas_call(
        regroup_kernel,
        out_shape=jax.ShapeDtypeStruct((parts, 1, shots, owners * rows), received.dtype),
        in_specs=[pl.BlockSpec(memory_space=pltpu.VMEM)],
        out_specs=pl.BlockSpec(memory_space=pl.ANY),
        scratch_shapes=[pltpu.SemaphoreType.DMA((owners,))],
        compiler_params=SMALL,
        name="regroup",
    )(received)


TREES = (
    ((4, 3), ((0, 1), (4, 7), (3, 5)), ((0, 2), (4, 6))),
    ((5, 2), ((1, 0), (5, 6), (2, 4)), ((1, 3), (5, 7))),
    ((3, 4), ((2, 0), (3, 7), (4, 5)), ((2, 6), (3, 1))),
    ((2, 5), ((3, 1), (2, 6), (5, 4)), ((3, 7), (2, 0))),
    ((5, 2), ((4, 0), (5, 1), (2, 3)), ((4, 6), (5, 7))),
    ((4, 3), ((5, 1), (4, 0), (3, 2)), ((5, 7), (4, 6))),
    ((2, 5), ((6, 4), (2, 1), (5, 3)), ((6, 7), (2, 0))),
    ((3, 4), ((7, 5), (3, 0), (4, 2)), ((7, 6), (3, 1))),
)


def broadcast(block, owner, beside):
    me = lax.axis_index("rows")

    def send(value, *pairs):
        return lax.ppermute(value, "rows", pairs)

    def branch(source):
        (one, two), first, second = TREES[source]

        def run(value):
            have = send(value, (source, one)) + send(value, (source, two))
            have = jnp.where(me == source, value, have)
            results = beside()
            return have + send(have, *first) + send(have, *second), results

        return run

    return lax.switch(owner, [branch(source) for source in range(len(TREES))], block)


def solve_eight(first, right_sides, panels, inverses, pivots):
    last = inverses.shape[0] - 1
    block, *owners = solve_first(pivots, right_sides, inverses)
    owners = [owner[0] for owner in owners]
    block, own = broadcast(block, owners[0], lambda: prepare(pivots, right_sides, panels, inverses))
    solved = [block]
    for panel in range(1, last):
        block = solve(own[panel - 1], solved)
        solved.append(broadcast(block, owners[panel], lambda: ())[0])
    block = solve(own[last - 1], solved)
    block, running = broadcast(block, owners[last], lambda: early_update(right_sides, panels, solved))
    solved.append(block)
    return last_update(first, pivots, running, panels, solved, len(TREES))


def complex_dot(matrix, vectors):
    half = vectors.shape[0] // 2
    return dot_t(vectors, matrix[0]) + dot_t(turned(vectors), matrix[1])


def solve_summed(me, owners, right_sides, panels, inverses, pivots):
    parts, local_rows, shots = right_sides.shape
    width = inverses.shape[-1]
    solved = []
    for panel in range(inverses.shape[0]):
        offset = lax.rem(pivots[panel], local_rows // width) * width
        rows = lax.dynamic_slice_in_dim(right_sides, offset, width, 1)
        rows = jnp.transpose(rows, (0, 2, 1)).reshape(parts * shots, width).astype(jnp.float32)
        factor = lax.dynamic_slice_in_dim(panels, offset, width, 1)
        for j, block in enumerate(solved):
            rows = rows - complex_dot(factor[:, :, j * width : (j + 1) * width], block)
        block = complex_dot(inverses[panel], rows.astype(jnp.bfloat16)).astype(jnp.bfloat16)
        block = jnp.where(me == owners[panel], block, jnp.zeros_like(block))
        solved.append(lax.psum(block, "rows"))
    return solved


def body(ranks, right_sides, panels, inverses, pivots):
    me = lax.axis_index("rows")
    per_device = right_sides.shape[1] // inverses.shape[-1]
    first = (me * per_device).reshape(1)
    if ranks == len(TREES):
        rows = solve_eight(first, right_sides, panels, inverses, pivots)
    else:
        owners = lax.div(pivots, jnp.full_like(pivots, per_device))
        solved = solve_summed(me, owners, right_sides, panels, inverses, pivots)
        running = early_update(right_sides, panels, solved[:-1])
        rows = last_update(first, pivots, running, panels, solved, ranks)
    received = lax.all_to_all(rows, "rows", split_axis=0, concat_axis=0, tiled=True)
    return regroup(received)


def solution(mesh):
    placed = (
        P(None, "rows", ("groups", "shots")),
        P(None, ("groups", "rows"), None),
        P("groups", None, None, None),
        P(),
    )
    return jax.shard_map(
        functools.partial(body, mesh.shape["rows"]),
        mesh=mesh,
        in_specs=placed,
        out_specs=P(None, "shots", ("groups", "rows"), None),
        check_vma=False,
    )
```

profile of v0, /device:TPU:0, one launch (start us, length us, event | category | flops | bytes accessed | tf_op | source)
XLA Modules:
  0.0 97.6 jit_solution(943085324906003250)
XLA Ops:
  0.0 2.4 %solve_first.1 = (bf16[256,256]{1,0:T(8,128)(2,1)S(1)}, s32[1]{0:T(128)}, s32[1]{0:T(128)}, s32[1]{0:T(128)}, s32[1]{0:T(128)}) custom-call(s32[4]{0:T(128)} %pivots_ref.3, bf16[2,2048,128]{2,1,0:T(8,128)(2,1)} %sides_ref.1, bf16[4,2,256,256]{3,2,1,0:T(8,128)(2,1)} %inverse_ref.1), custom_call_target="tpu_custom_call" | custom-call | tf_op jit(solution)/shard_map/solve_first/pallas_call | solution.py:46
  3.1 17.5 %conditional.4 = (bf16[256,256]{1,0:T(8,128)(2,1)S(1)}, bf16[1280,256]{1,0:T(8,128)(2,1)S(1)}, bf16[1792,256]{1,0:T(8,128)(2,1)}, bf16[2304,256]{1,0:T(8,128)(2,1)S(1)}) conditional(s32[]{:T(128)} %bitcast.2, (s32[]{:T(128)}, bf16[256,256]{1,0:T(8,128)(2,1)S(1)}, s32[4]{0:T(128)S(1)}, ...), branch_computations={%region_0.1_spmd, %region_1.2_spmd, %region_2.3_spmd, %region_3.4_... | conditional | flops 262145 | bytes 3145930 | solution.py:271
  3.1 6.0 %collective-permute-start = (bf16[256,256]{1,0:T(8,128)(2,1)S(1)}, bf16[256,256]{1,0:T(8,128)(2,1)S(1)}, u32[]{:S(2)}, u32[]{:S(2)}) collective-permute-start(bf16[256,256]{1,0:T(8,128)(2,1)S(1)} %get-tuple-element.280), channel_id=1, source_target_pairs={{0,8},{1,9},{16,24},{17,25}} | collective-permute-start | bytes 393224 | tf_op jit(solution)/shard_map/cond/branch_0_fun/ppermute | solution.py:258
  9.1 1.3 %collective-permute-start.1 = (bf16[256,256]{1,0:T(8,128)(2,1)S(1)}, bf16[256,256]{1,0:T(8,128)(2,1)S(1)}, u32[]{:S(2)}, u32[]{:S(2)}) collective-permute-start(bf16[256,256]{1,0:T(8,128)(2,1)S(1)} %get-tuple-element.280), channel_id=1, source_target_pairs={{0,6},{1,7},{16,22},{17,23}} | collective-permute-start | bytes 393224 | tf_op jit(solution)/shard_map/cond/branch_0_fun/ppermute | solution.py:258
  10.4 2.6 %collective-permute-done = bf16[256,256]{1,0:T(8,128)(2,1)S(1)} collective-permute-done((bf16[256,256]{1,0:T(8,128)(2,1)S(1)}, bf16[256,256]{1,0:T(8,128)(2,1)S(1)}, u32[]{:S(2)}, u32[]{:S(2)}) %collective-permute-start) | collective-permute-done | bytes 131104 | tf_op jit(solution)/shard_map/cond/branch_0_fun/ppermute | solution.py:258
  12.9 1.7 %collective-permute-done.1 = bf16[256,256]{1,0:T(8,128)(2,1)S(1)} collective-permute-done((bf16[256,256]{1,0:T(8,128)(2,1)S(1)}, bf16[256,256]{1,0:T(8,128)(2,1)S(1)}, u32[]{:S(2)}, u32[]{:S(2)}) %collective-permute-start.1) | collective-permute-done | bytes 131104 | tf_op jit(solution)/shard_map/cond/branch_0_fun/ppermute | solution.py:258
  14.6 1.3 %collective-permute-start.2 = (bf16[256,256]{1,0:T(8,128)(2,1)S(1)}, bf16[256,256]{1,0:T(8,128)(2,1)S(1)}, u32[]{:S(2)}, u32[]{:S(2)}) collective-permute-start(bf16[256,256]{1,0:T(8,128)(2,1)S(1)} %add_select_fusion), channel_id=1, source_target_pairs={{0,2},{8,14},{6,10},{1,3},{9,15},{7,11},{16,18},{24,30},{22,26},{1... | collective-permute-start | bytes 393224 | tf_op jit(solution)/shard_map/cond/branch_0_fun/ppermute | solution.py:258
  15.9 1.3 %collective-permute-start.3 = (bf16[256,256]{1,0:T(8,128)(2,1)S(1)}, bf16[256,256]{1,0:T(8,128)(2,1)S(1)}, u32[]{:S(2)}, u32[]{:S(2)}) collective-permute-start(bf16[256,256]{1,0:T(8,128)(2,1)S(1)} %add_select_fusion), channel_id=1, source_target_pairs={{0,4},{8,12},{1,5},{9,13},{16,20},{24,28},{17,21},{25,29}} | collective-permute-start | bytes 393224 | tf_op jit(solution)/shard_map/cond/branch_0_fun/ppermute | solution.py:258
  17.2 3.2 %prepare.8 = (bf16[1280,256]{1,0:T(8,128)(2,1)S(1)}, bf16[1792,256]{1,0:T(8,128)(2,1)}, bf16[2304,256]{1,0:T(8,128)(2,1)S(1)}) custom-call(s32[4]{0:T(128)S(1)} %get-tuple-element.281.pivots_ref, bf16[4,2,256,256]{3,2,1,0:T(8,128)(2,1)S(1)} %get-tuple-element.282.inverse_ref, bf16[2,2048,128]{2,1,0:T(8,128)(2,1)S(1)} %get-tuple-element.290.refs_0_.refs_1_.refs_2_, ...), custom_call_target="tpu_custom_call" | custom-call | tf_op jit(solution)/shard_map/cond/branch_0_fun/prepare/pallas_call | solution.py:88
  21.8 16.7 %conditional.5 = (bf16[256,256]{1,0:T(8,128)(2,1)S(1)}) conditional(s32[]{:T(128)} %bitcast.3, (s32[]{:T(128)}, bf16[256,256]{1,0:T(8,128)(2,1)S(1)}) %tuple.118, (s32[]{:T(128)}, bf16[256,256]{1,0:T(8,128)(2,1)S(1)}) %tuple.118, (s32[]{:T(128)}, bf16[256,256]{1,0:T(8,128)(2,1)S(1)}) %tuple.118, (s32[]{:T(128)}, ...), branch_computations={%region_8.9_spmd, %region_9.10_spmd, %region_10.11_spmd, %region_1... | conditional | flops 262145 | bytes 3145906 | solution.py:271
  22.6 1.3 %collective-permute-start.61 = (bf16[256,256]{1,0:T(8,128)(2,1)S(1)}, bf16[256,256]{1,0:T(8,128)(2,1)}, u32[]{:S(2)}, u32[]{:S(2)}) collective-permute-start(bf16[256,256]{1,0:T(8,128)(2,1)S(1)} %get-tuple-element.382), channel_id=1, source_target_pairs={{14,8},{15,9},{30,24},{31,25}} | collective-permute-start | bytes 393224 | tf_op jit(solution)/shard_map/cond/branch_7_fun/ppermute | solution.py:258
  23.9 0.9 add_select_fusion.15
  24.9 1.3 %collective-permute-start.62 = (bf16[256,256]{1,0:T(8,128)(2,1)S(1)}, bf16[256,256]{1,0:T(8,128)(2,1)S(1)}, u32[]{:S(2)}, u32[]{:S(2)}) collective-permute-start(bf16[256,256]{1,0:T(8,128)(2,1)S(1)} %add_select_fusion.15), channel_id=1, source_target_pairs={{14,10},{6,0},{8,4},{15,11},{7,1},{9,5},{30,26},{22,16},{24,20},{3... | collective-permute-start | bytes 393224 | tf_op jit(solution)/shard_map/cond/branch_7_fun/ppermute | solution.py:258
  26.9 11.6 %collective-permute-done.62 = bf16[256,256]{1,0:T(8,128)(2,1)S(1)} collective-permute-done((bf16[256,256]{1,0:T(8,128)(2,1)S(1)}, bf16[256,256]{1,0:T(8,128)(2,1)S(1)}, u32[]{:S(2)}, u32[]{:S(2)}) %collective-permute-start.62) | collective-permute-done | bytes 131104 | tf_op jit(solution)/shard_map/cond/branch_7_fun/ppermute | solution.py:258
  39.7 14.3 %conditional.6 = (bf16[256,256]{1,0:T(8,128)(2,1)S(1)}) conditional(s32[]{:T(128)} %bitcast.4, (s32[]{:T(128)}, bf16[256,256]{1,0:T(8,128)(2,1)S(1)}) %tuple.119, (s32[]{:T(128)}, bf16[256,256]{1,0:T(8,128)(2,1)S(1)}) %tuple.119, (s32[]{:T(128)}, bf16[256,256]{1,0:T(8,128)(2,1)S(1)}) %tuple.119, (s32[]{:T(128)}, ...), branch_computations={%region_16.17_spmd, %region_17.18_spmd, %region_18.19_spmd, %regio... | conditional | flops 262145 | bytes 3145906 | solution.py:271
  41.2 1.3 %collective-permute-start.94 = (bf16[256,256]{1,0:T(8,128)(2,1)S(1)}, bf16[256,256]{1,0:T(8,128)(2,1)S(1)}, u32[]{:S(2)}, u32[]{:S(2)}) collective-permute-start(bf16[256,256]{1,0:T(8,128)(2,1)S(1)} %add_select_fusion.23), channel_id=1, source_target_pairs={{14,10},{6,0},{8,4},{15,11},{7,1},{9,5},{30,26},{22,16},{24,20},{3... | collective-permute-start | bytes 393224 | tf_op jit(solution)/shard_map/cond/branch_7_fun/ppermute | solution.py:258
  43.1 10.7 %collective-permute-done.94 = bf16[256,256]{1,0:T(8,128)(2,1)S(1)} collective-permute-done((bf16[256,256]{1,0:T(8,128)(2,1)S(1)}, bf16[256,256]{1,0:T(8,128)(2,1)S(1)}, u32[]{:S(2)}, u32[]{:S(2)}) %collective-permute-start.94) | collective-permute-done | bytes 131104 | tf_op jit(solution)/shard_map/cond/branch_7_fun/ppermute | solution.py:258
  55.3 14.7 %conditional.7 = (bf16[256,256]{1,0:T(8,128)(2,1)S(1)}, f32[256,2048]{1,0:T(8,128)S(1)}) conditional(s32[]{:T(128)} %bitcast.1, (s32[]{:T(128)}, bf16[256,256]{1,0:T(8,128)(2,1)S(1)}, bf16[2,2048,128]{2,1,0:T(8,128)(2,1)S(1)}, bf16[2,2048,1024]{2,1,0:T(8,128)(2,1)}, bf16[256,256]{1,0:T(8,128)(2,1)S(1)}, ...), branch_computations={%region_24.25_spmd, %region_25.26_spmd, %region_26.27_spmd, %regio... | conditional | flops 262145 | bytes 3145914 | solution.py:271
  57.5 1.3 %collective-permute-start.111 = (bf16[256,256]{1,0:T(8,128)(2,1)S(1)}, bf16[256,256]{1,0:T(8,128)(2,1)S(1)}, u32[]{:S(2)}, u32[]{:S(2)}) collective-permute-start(bf16[256,256]{1,0:T(8,128)(2,1)S(1)} %add_select_fusion.27), channel_id=1, source_target_pairs={{6,14},{4,0},{7,15},{5,1},{22,30},{20,16},{23,31},{21,17}} | collective-permute-start | bytes 393224 | tf_op jit(solution)/shard_map/cond/branch_3_fun/ppermute | solution.py:258
  58.8 4.5 %early_update.11 = f32[256,2048]{1,0:T(8,128)S(1)} custom-call(bf16[2,2048,128]{2,1,0:T(8,128)(2,1)S(1)} %get-tuple-element.422.sides_ref, bf16[2,2048,1024]{2,1,0:T(8,128)(2,1)} %get-tuple-element.423.panel_ref, bf16[256,256]{1,0:T(8,128)(2,1)S(1)} %get-tuple-element.424.refs_0_, bf16[256,256]{1,0:T(8,128)(2,1)S(1)} %get-tuple-element.425.refs_1_, ...), custom_call_target="tpu_custom_call" | custom-call | tf_op jit(solution)/shard_map/cond/branch_3_fun/early_update/pallas_call | solution.py:153
  63.3 6.7 %collective-permute-done.111 = bf16[256,256]{1,0:T(8,128)(2,1)S(1)} collective-permute-done((bf16[256,256]{1,0:T(8,128)(2,1)S(1)}, bf16[256,256]{1,0:T(8,128)(2,1)S(1)}, u32[]{:S(2)}, u32[]{:S(2)}) %collective-permute-start.111) | collective-permute-done | bytes 131104 | tf_op jit(solution)/shard_map/cond/branch_3_fun/ppermute | solution.py:258
  70.1 3.9 %last_update.1 = bf16[8,2,16,2048]{3,2,1,0:T(8,128)(2,1)} custom-call(s32[4]{0:T(128)S(1)} %copy-done.3, s32[1]{0:T(128)} %bitcast.first_ref, f32[256,2048]{1,0:T(8,128)S(1)} %get-tuple-element.475.running_ref, bf16[2,2048,1024]{2,1,0:T(8,128)(2,1)} %panel_ref.1, bf16[256,256]{1,0:T(8,128)(2,1)S(1)} %get-tuple-element.470.refs_0_, ...), custom_call_target="tpu_custom_call" | custom-call | tf_op jit(solution)/shard_map/last_update/pallas_call | solution.py:199
  73.9 22.5 %all_to_all.5.rows_ref = bf16[8,2,16,2048]{3,2,1,0:T(8,128)(2,1)S(1)} all-to-all(bf16[8,2,16,2048]{3,2,1,0:T(8,128)(2,1)} %last_update.1), channel_id=1, replica_groups=mesh['groups'=2,'rows'=8,'shots'=2] {'rows'}, dimensions={0} | all-to-all | bytes 2097152 | tf_op jit(solution)/shard_map/all_to_all | solution.py:322
  96.4 1.0 %regroup.1 = bf16[2,1,16,16384]{3,2,1,0:T(8,128)(2,1)} custom-call(bf16[8,2,16,2048]{3,2,1,0:T(8,128)(2,1)S(1)} %all_to_all.5.rows_ref), custom_call_target="tpu_custom_call" | custom-call | tf_op jit(solution)/shard_map/regroup/pallas_call | solution.py:231
  (37 shorter events, 7.5 us)
Async XLA Ops:
  0.0 3.0 %copy-start = (bf16[2,2048,128]{2,1,0:T(8,128)(2,1)S(1)}, bf16[2,2048,128]{2,1,0:T(8,128)(2,1)}, u32[]{:S(2)}) copy-start(bf16[2,2048,128]{2,1,0:T(8,128)(2,1)} %sides_ref.1) | copy-start | bytes 3145732
  0.0 3.0 %copy-start.1 = (bf16[4,2,256,256]{3,2,1,0:T(8,128)(2,1)S(1)}, bf16[4,2,256,256]{3,2,1,0:T(8,128)(2,1)}, u32[]{:S(2)}) copy-start(bf16[4,2,256,256]{3,2,1,0:T(8,128)(2,1)} %inverse_ref.1) | copy-start | bytes 3145732
  0.0 3.1 %copy-start.3 = (s32[4]{0:T(128)S(1)}, s32[4]{0:T(128)}, u32[]{:S(2)}) copy-start(s32[4]{0:T(128)} %pivots_ref.3) | copy-start | bytes 52
  3.1 9.8 %collective-permute-start = (bf16[256,256]{1,0:T(8,128)(2,1)S(1)}, bf16[256,256]{1,0:T(8,128)(2,1)S(1)}, u32[]{:S(2)}, u32[]{:S(2)}) collective-permute-start(bf16[256,256]{1,0:T(8,128)(2,1)S(1)} %get-tuple-element.280), channel_id=1, source_target_pairs={{0,8},{1,9},{16,24},{17,25}} | collective-permute-start | bytes 393224 | tf_op jit(solution)/shard_map/cond/branch_0_fun/ppermute | solution.py:258
  9.1 5.5 %collective-permute-start.1 = (bf16[256,256]{1,0:T(8,128)(2,1)S(1)}, bf16[256,256]{1,0:T(8,128)(2,1)S(1)}, u32[]{:S(2)}, u32[]{:S(2)}) collective-permute-start(bf16[256,256]{1,0:T(8,128)(2,1)S(1)} %get-tuple-element.280), channel_id=1, source_target_pairs={{0,6},{1,7},{16,22},{17,23}} | collective-permute-start | bytes 393224 | tf_op jit(solution)/shard_map/cond/branch_0_fun/ppermute | solution.py:258
  14.6 5.9 %collective-permute-start.2 = (bf16[256,256]{1,0:T(8,128)(2,1)S(1)}, bf16[256,256]{1,0:T(8,128)(2,1)S(1)}, u32[]{:S(2)}, u32[]{:S(2)}) collective-permute-start(bf16[256,256]{1,0:T(8,128)(2,1)S(1)} %add_select_fusion), channel_id=1, source_target_pairs={{0,2},{8,14},{6,10},{1,3},{9,15},{7,11},{16,18},{24,30},{22,26},{1... | collective-permute-start | bytes 393224 | tf_op jit(solution)/shard_map/cond/branch_0_fun/ppermute | solution.py:258
  15.9 4.6 %collective-permute-start.3 = (bf16[256,256]{1,0:T(8,128)(2,1)S(1)}, bf16[256,256]{1,0:T(8,128)(2,1)S(1)}, u32[]{:S(2)}, u32[]{:S(2)}) collective-permute-start(bf16[256,256]{1,0:T(8,128)(2,1)S(1)} %add_select_fusion), channel_id=1, source_target_pairs={{0,4},{8,12},{1,5},{9,13},{16,20},{24,28},{17,21},{25,29}} | collective-permute-start | bytes 393224 | tf_op jit(solution)/shard_map/cond/branch_0_fun/ppermute | solution.py:258
  21.8 16.7 %copy-start.2 = (bf16[1792,256]{1,0:T(8,128)(2,1)S(1)}, bf16[1792,256]{1,0:T(8,128)(2,1)}, u32[]{:S(2)}) copy-start(bf16[1792,256]{1,0:T(8,128)(2,1)} %get-tuple-element.474.own_ref) | copy-start | bytes 2752516
  21.8 2.1 %collective-permute-start.60 = (bf16[256,256]{1,0:T(8,128)(2,1)S(1)}, bf16[256,256]{1,0:T(8,128)(2,1)S(1)}, u32[]{:S(2)}, u32[]{:S(2)}) collective-permute-start(bf16[256,256]{1,0:T(8,128)(2,1)S(1)} %get-tuple-element.382), channel_id=1, source_target_pairs={{14,6},{15,7},{30,22},{31,23}} | collective-permute-start | bytes 393224 | tf_op jit(solution)/shard_map/cond/branch_7_fun/ppermute | solution.py:258
  22.6 1.3 %collective-permute-start.61 = (bf16[256,256]{1,0:T(8,128)(2,1)S(1)}, bf16[256,256]{1,0:T(8,128)(2,1)}, u32[]{:S(2)}, u32[]{:S(2)}) collective-permute-start(bf16[256,256]{1,0:T(8,128)(2,1)S(1)} %get-tuple-element.382), channel_id=1, source_target_pairs={{14,8},{15,9},{30,24},{31,25}} | collective-permute-start | bytes 393224 | tf_op jit(solution)/shard_map/cond/branch_7_fun/ppermute | solution.py:258
  24.9 13.5 %collective-permute-start.62 = (bf16[256,256]{1,0:T(8,128)(2,1)S(1)}, bf16[256,256]{1,0:T(8,128)(2,1)S(1)}, u32[]{:S(2)}, u32[]{:S(2)}) collective-permute-start(bf16[256,256]{1,0:T(8,128)(2,1)S(1)} %add_select_fusion.15), channel_id=1, source_target_pairs={{14,10},{6,0},{8,4},{15,11},{7,1},{9,5},{30,26},{22,16},{24,20},{3... | collective-permute-start | bytes 393224 | tf_op jit(solution)/shard_map/cond/branch_7_fun/ppermute | solution.py:258
  26.2 12.2 %collective-permute-start.63 = (bf16[256,256]{1,0:T(8,128)(2,1)S(1)}, bf16[256,256]{1,0:T(8,128)(2,1)S(1)}, u32[]{:S(2)}, u32[]{:S(2)}) collective-permute-start(bf16[256,256]{1,0:T(8,128)(2,1)S(1)} %add_select_fusion.15), channel_id=1, source_target_pairs={{14,12},{6,2},{15,13},{7,3},{30,28},{22,18},{31,29},{23,19}} | collective-permute-start | bytes 393224 | tf_op jit(solution)/shard_map/cond/branch_7_fun/ppermute | solution.py:258
  39.8 1.4 %collective-permute-start.92 = (bf16[256,256]{1,0:T(8,128)(2,1)S(1)}, bf16[256,256]{1,0:T(8,128)(2,1)S(1)}, u32[]{:S(2)}, u32[]{:S(2)}) collective-permute-start(bf16[256,256]{1,0:T(8,128)(2,1)S(1)} %get-tuple-element.398), channel_id=1, source_target_pairs={{14,6},{15,7},{30,22},{31,23}} | collective-permute-start | bytes 393224 | tf_op jit(solution)/shard_map/cond/branch_7_fun/ppermute | solution.py:258
  40.4 0.7 collective-permute-start.93
  41.2 12.7 %collective-permute-start.94 = (bf16[256,256]{1,0:T(8,128)(2,1)S(1)}, bf16[256,256]{1,0:T(8,128)(2,1)S(1)}, u32[]{:S(2)}, u32[]{:S(2)}) collective-permute-start(bf16[256,256]{1,0:T(8,128)(2,1)S(1)} %add_select_fusion.23), channel_id=1, source_target_pairs={{14,10},{6,0},{8,4},{15,11},{7,1},{9,5},{30,26},{22,16},{24,20},{3... | collective-permute-start | bytes 393224 | tf_op jit(solution)/shard_map/cond/branch_7_fun/ppermute | solution.py:258
  42.5 11.4 %collective-permute-start.95 = (bf16[256,256]{1,0:T(8,128)(2,1)S(1)}, bf16[256,256]{1,0:T(8,128)(2,1)S(1)}, u32[]{:S(2)}, u32[]{:S(2)}) collective-permute-start(bf16[256,256]{1,0:T(8,128)(2,1)S(1)} %add_select_fusion.23), channel_id=1, source_target_pairs={{14,12},{6,2},{15,13},{7,3},{30,28},{22,18},{31,29},{23,19}} | collective-permute-start | bytes 393224 | tf_op jit(solution)/shard_map/cond/branch_7_fun/ppermute | solution.py:258
  55.4 1.4 %collective-permute-start.108 = (bf16[256,256]{1,0:T(8,128)(2,1)S(1)}, bf16[256,256]{1,0:T(8,128)(2,1)S(1)}, u32[]{:S(2)}, u32[]{:S(2)}) collective-permute-start(bf16[256,256]{1,0:T(8,128)(2,1)S(1)} %get-tuple-element.421), channel_id=1, source_target_pairs={{6,4},{7,5},{22,20},{23,21}} | collective-permute-start | bytes 393224 | tf_op jit(solution)/shard_map/cond/branch_3_fun/ppermute | solution.py:258
  56.0 0.7 collective-permute-start.109
  56.8 6.5 %collective-permute-start.110 = (bf16[256,256]{1,0:T(8,128)(2,1)S(1)}, bf16[256,256]{1,0:T(8,128)(2,1)S(1)}, u32[]{:S(2)}, u32[]{:S(2)}) collective-permute-start(bf16[256,256]{1,0:T(8,128)(2,1)S(1)} %add_select_fusion.27), channel_id=1, source_target_pairs={{6,2},{4,12},{10,8},{7,3},{5,13},{11,9},{22,18},{20,28},{26,24},{2... | collective-permute-start | bytes 393224 | tf_op jit(solution)/shard_map/cond/branch_3_fun/ppermute | solution.py:258
  57.5 12.6 %collective-permute-start.111 = (bf16[256,256]{1,0:T(8,128)(2,1)S(1)}, bf16[256,256]{1,0:T(8,128)(2,1)S(1)}, u32[]{:S(2)}, u32[]{:S(2)}) collective-permute-start(bf16[256,256]{1,0:T(8,128)(2,1)S(1)} %add_select_fusion.27), channel_id=1, source_target_pairs={{6,14},{4,0},{7,15},{5,1},{22,30},{20,16},{23,31},{21,17}} | collective-permute-start | bytes 393224 | tf_op jit(solution)/shard_map/cond/branch_3_fun/ppermute | solution.py:258
where the time goes:
time: 99.1 us; the launch traced here: 97.6 us
  waiting for transfers between devices  33.2 us (34%)
  blocking collectives  22.5 us (23%)
  starting transfers between devices  20.5 us (21%)
  Pallas kernels  16.9 us (17%)
  between operations  2.8 us (3%)
  other arithmetic  1.08 us (1%)
    ppermute x16, waiting for transfers between devices, send(): return lax.ppermute(value, 'rows', pairs)  33.2 us
    all_to_all x1, blocking collectives, body(): lax.all_to_all(rows, 'rows', split_axis=0, concat_axis=0, tiled=True)  22.5 us
    ppermute x16, starting transfers between devices, send(): return lax.ppermute(value, 'rows', pairs)  20.5 us
    pallas_call x1, Pallas kernels, early_update(): pl.pallas_call(early_kernel, out_shape=jax.ShapeDtypeStruct((height, loca...  4.54 us
    pallas_call x1, Pallas kernels, last_update(): pl.pallas_call(functools.partial(last_kernel, owners), out_shape=jax.Shap...  3.88 us
    pallas_call x1, Pallas kernels, prepare(): pl.pallas_call(functools.partial(prepare_kernel, count), out_shape=[jax.S...  3.25 us
    pallas_call x1, Pallas kernels, solve_first(): pl.pallas_call(functools.partial(first_kernel, per_device), out_shape=[ja...  2.37 us
  transfers between devices with their start and end apart: 16, of which 5 were waited for; matrix products, arithmetic and copies ran while one was open for 0% of the time, Pallas kernels for 8%

commit v1 on v0

--- a/solution.py
+++ b/solution.py
@@ -9,8 +9,9 @@
 
 CONTRACT_LAST = (((1,), (1,)), ((), ()))
 
-BESIDE_PANELS = pltpu.CompilerParams(vmem_limit_bytes=57 * 1024 * 1024)
+BESIDE_PANELS = pltpu.CompilerParams(vmem_limit_bytes=40 * 1024 * 1024)
 TILES = 4
+RANKS = 8
 SMALL = pltpu.CompilerParams(vmem_limit_bytes=16 * 1024 * 1024)
 
 
@@ -62,9 +63,10 @@
     )(pivots, right_sides, inverses)
 
 
-def prepare_kernel(count, pivots_ref, inverse_ref, *refs):
-    sides_refs, panel_refs, out_refs = refs[: count - 1], refs[count - 1 : 2 * count - 2], refs[2 * count - 2 :]
-    for panel, (sides_ref, panel_ref, out_ref) in enumerate(zip(sides_refs, panel_refs, out_refs), 1):
+def prepare_kernel(panels, pivots_ref, inverse_ref, *refs):
+    count = len(panels)
+    sides_refs, panel_refs, out_refs = refs[:count], refs[count : 2 * count], refs[2 * count :]
+    for panel, sides_ref, panel_ref, out_ref in zip(panels, sides_refs, panel_refs, out_refs):
         parts, width, shots = sides_ref.shape
         for part in range(parts):
             out_ref[part * width : (part + 1) * width] = inverse_ref[panel, part]
@@ -76,29 +78,29 @@
             out_ref[start + n * width : start + (n + 1) * width] = panel_ref[p, :, j * width : (j + 1) * width]
 
 
-def prepare(pivots, right_sides, panels, inverses):
+def prepare(numbers, pivots, right_sides, panels, inverses):
     parts, local_rows, shots = right_sides.shape
-    count, width = inverses.shape[0], inverses.shape[-1]
+    width = inverses.shape[-1]
     per_device = local_rows // width
 
     def slot(panel):
         return lambda i, pivots_ref: (0, lax.rem(pivots_ref[panel], per_device), 0)
 
-    shapes = [(parts * (shots + (panel + 1) * width), width) for panel in range(1, count)]
-    return pl.pallas_call(
-        functools.partial(prepare_kernel, count),
+    shapes = [(parts * (shots + (panel + 1) * width), width) for panel in numbers]
+    return pl.pallas_call(
+        functools.partial(prepare_kernel, numbers),
         out_shape=[jax.ShapeDtypeStruct(shape, jnp.bfloat16) for shape in shapes],
         grid_spec=pltpu.PrefetchScalarGridSpec(
             num_scalar_prefetch=1,
             grid=(1,),
             in_specs=[pl.BlockSpec(inverses.shape, lambda i, *_: (0, 0, 0, 0))]
-            + [pl.BlockSpec((parts, width, shots), slot(panel)) for panel in range(1, count)]
-            + [pl.BlockSpec((parts, width, panel * width), slot(panel)) for panel in range(1, count)],
+            + [pl.BlockSpec((parts, width, shots), slot(panel)) for panel in numbers]
+            + [pl.BlockSpec((parts, width, panel * width), slot(panel)) for panel in numbers],
             out_specs=[pl.BlockSpec(shape, lambda i, *_: (0, 0)) for shape in shapes],
         ),
         compiler_params=BESIDE_PANELS,
         name="prepare",
-    )(pivots, inverses, *[right_sides] * (count - 1), *[panels] * (count - 1))
+    )(pivots, inverses, *[right_sides] * len(numbers), *[panels] * len(numbers))
 
 
 def solve_kernel(own_ref, *refs):
@@ -131,7 +133,7 @@
 
 
 def early_kernel(sides_ref, panel_ref, *refs):
-    solved_refs, (out_ref, real_ref, imag_ref) = refs[:-3], refs[-3:]
+    solved_refs, (out_ref, panel_out_ref, real_ref, imag_ref) = refs[:-4], refs[-4:]
     width = solved_refs[0].shape[1]
 
     @pl.when(pl.program_id(0) == 0)
@@ -141,25 +143,34 @@
             real_ref[:, j * width : (j + 1) * width] = solved
             imag_ref[:, j * width : (j + 1) * width] = turned(solved)
 
-    values = transposed_sides(sides_ref) - dot_t(real_ref[...], panel_ref[0])
-    out_ref[...] = values - dot_t(imag_ref[...], panel_ref[1])
+    columns = len(solved_refs) * width
+    panel_out_ref[...] = panel_ref[:, :, columns:]
+    values = transposed_sides(sides_ref) - dot_t(real_ref[...], panel_ref[0, :, :columns])
+    out_ref[...] = values - dot_t(imag_ref[...], panel_ref[1, :, :columns])
 
 
 def early_update(right_sides, panels, solved):
     parts, local_rows, shots = right_sides.shape
     height, width = solved[0].shape
     columns = len(solved) * width
+    rest = panels.shape[2] - columns
     tile = TILES * width if local_rows % (TILES * width) == 0 else width
     return pl.pallas_call(
         early_kernel,
-        out_shape=jax.ShapeDtypeStruct((height, local_rows), jnp.float32),
+        out_shape=[
+            jax.ShapeDtypeStruct((height, local_rows), jnp.float32),
+            jax.ShapeDtypeStruct((parts, local_rows, rest), jnp.bfloat16),
+        ],
         grid=(local_rows // tile,),
         in_specs=[
             pl.BlockSpec((parts, tile, shots), lambda i: (0, i, 0)),
-            pl.BlockSpec((parts, tile, columns), lambda i: (0, i, 0)),
+            pl.BlockSpec((parts, tile, panels.shape[2]), lambda i: (0, i, 0)),
         ]
         + [pl.BlockSpec((height, width), lambda i: (0, 0)) for _ in solved],
-        out_specs=pl.BlockSpec((height, tile), lambda i: (0, i)),
+        out_specs=[
+            pl.BlockSpec((height, tile), lambda i: (0, i)),
+            pl.BlockSpec((parts, tile, rest), lambda i: (0, i, 0)),
+        ],
         scratch_shapes=[pltpu.VMEM((height, columns), jnp.bfloat16)] * 2,
         compiler_params=BESIDE_PANELS,
         name="early_update",
@@ -168,50 +179,43 @@
 
 def last_kernel(owners, pivots_ref, first_ref, running_ref, panel_ref, *refs):
     solved_refs, out_ref = refs[:-1], refs[-1]
-    rows = running_ref.shape[1]
+    height, rows = running_ref.shape
     width = solved_refs[0].shape[1]
-    solved = solved_refs[-1][...]
-    values = running_ref[...] - dot_t(solved, panel_ref[0]) - dot_t(turned(solved), panel_ref[1])
-    shots = values.shape[0] // 2
+    shots = height // 2
     each = shots // owners
 
-    def write(block, columns):
+    def write(values, k):
         for part in range(2):
             for owner in range(owners):
                 start = part * shots + owner * each
-                out_ref[owner, part, :, columns] = block[start : start + each]
-
-    write(values.astype(jnp.bfloat16), slice(None))
-    first = first_ref[0] + pl.program_id(0) * (rows // width)
-    for j, solved_ref in enumerate(solved_refs):
-        for k in range(rows // width):
-
-            @pl.when(pivots_ref[j] == first + k)
+                out_ref[owner, part, :, k * width : (k + 1) * width] = values[start : start + each]
+
+    solved = solved_refs[-1][...]
+    around = turned(solved)
+    for k in range(rows // width):
+        columns = slice(k * width, (k + 1) * width)
+        values = running_ref[:, columns] - dot_t(solved, panel_ref[0, columns])
+        write((values - dot_t(around, panel_ref[1, columns])).astype(jnp.bfloat16), k)
+        for j, solved_ref in enumerate(solved_refs):
+
+            @pl.when(pivots_ref[j] == first_ref[0] + k)
             def _():
-                write(solved_ref[...], slice(k * width, (k + 1) * width))
-
-
-def last_update(first, pivots, running, panels, solved, owners):
-    parts, local_rows, columns = panels.shape
+                write(solved_ref[...], k)
+
+
+def last_update(first, pivots, running, panel, solved, owners):
+    parts, local_rows, _ = panel.shape
     height, width = solved[0].shape
     each = height // parts // owners
-    tile = TILES * width if local_rows % (TILES * width) == 0 else width
     return pl.pallas_call(
         functools.partial(last_kernel, owners),
         out_shape=jax.ShapeDtypeStruct((owners, parts, each, local_rows), jnp.bfloat16),
-        grid_spec=pltpu.PrefetchScalarGridSpec(
-            num_scalar_prefetch=2,
-            grid=(local_rows // tile,),
-            in_specs=[
-                pl.BlockSpec((height, tile), lambda i, *_: (0, i)),
-                pl.BlockSpec((parts, tile, width), lambda i, *_: (0, i, columns // width - 1)),
-            ]
-            + [pl.BlockSpec(block.shape, lambda i, *_: (0, 0)) for block in solved],
-            out_specs=pl.BlockSpec((owners, parts, each, tile), lambda i, *_: (0, 0, 0, i)),
-        ),
-        compiler_params=BESIDE_PANELS,
+        in_specs=[pl.BlockSpec(memory_space=pltpu.SMEM)] * 2
+        + [pl.BlockSpec(memory_space=pltpu.VMEM)] * (2 + len(solved)),
+        out_specs=pl.BlockSpec(memory_space=pltpu.VMEM),
+        compiler_params=SMALL,
         name="last_update",
-    )(pivots, first, running, panels, *solved)
+    )(pivots, first, running, panel, *solved)
 
 
 def regroup_kernel(rows_ref, out_ref, sems):
@@ -239,51 +243,41 @@
     )(received)
 
 
-TREES = (
-    ((4, 3), ((0, 1), (4, 7), (3, 5)), ((0, 2), (4, 6))),
-    ((5, 2), ((1, 0), (5, 6), (2, 4)), ((1, 3), (5, 7))),
-    ((3, 4), ((2, 0), (3, 7), (4, 5)), ((2, 6), (3, 1))),
-    ((2, 5), ((3, 1), (2, 6), (5, 4)), ((3, 7), (2, 0))),
-    ((5, 2), ((4, 0), (5, 1), (2, 3)), ((4, 6), (5, 7))),
-    ((4, 3), ((5, 1), (4, 0), (3, 2)), ((5, 7), (4, 6))),
-    ((2, 5), ((6, 4), (2, 1), (5, 3)), ((6, 7), (2, 0))),
-    ((3, 4), ((7, 5), (3, 0), (4, 2)), ((7, 6), (3, 1))),
-)
-
-
 def broadcast(block, owner, beside):
     me = lax.axis_index("rows")
 
-    def send(value, *pairs):
-        return lax.ppermute(value, "rows", pairs)
-
     def branch(source):
-        (one, two), first, second = TREES[source]
-
         def run(value):
-            have = send(value, (source, one)) + send(value, (source, two))
-            have = jnp.where(me == source, value, have)
+            early = [lax.ppermute(value, "rows", [(source, source ^ step)]) for step in (4, 1)]
+            have = jnp.where(me == source, value, early[0] + early[1])
             results = beside()
-            return have + send(have, *first) + send(have, *second), results
+            corner = [source ^ step for step in (0, 1, 4, 5)]
+            third = lax.ppermute(have, "rows", sorted((device, device ^ 2) for device in corner))
+            fourth = lax.ppermute(have, "rows", [(source ^ 4, source ^ 5), (source, source ^ 7)])
+            return have + third + fourth, results
 
         return run
 
-    return lax.switch(owner, [branch(source) for source in range(len(TREES))], block)
+    return lax.switch(owner, [branch(source) for source in range(RANKS)], block)
 
 
 def solve_eight(first, right_sides, panels, inverses, pivots):
     last = inverses.shape[0] - 1
     block, *owners = solve_first(pivots, right_sides, inverses)
     owners = [owner[0] for owner in owners]
-    block, own = broadcast(block, owners[0], lambda: prepare(pivots, right_sides, panels, inverses))
+    block, own = broadcast(block, owners[0], lambda: prepare((1,), pivots, right_sides, panels, inverses))
     solved = [block]
     for panel in range(1, last):
-        block = solve(own[panel - 1], solved)
-        solved.append(broadcast(block, owners[panel], lambda: ())[0])
+        block = solve(own[-1], solved)
+        block, more = broadcast(
+            block, owners[panel], lambda: prepare((panel + 1,), pivots, right_sides, panels, inverses)
+        )
+        own = own + more
+        solved.append(block)
     block = solve(own[last - 1], solved)
-    block, running = broadcast(block, owners[last], lambda: early_update(right_sides, panels, solved))
+    block, (running, panel) = broadcast(block, owners[last], lambda: early_update(right_sides, panels, solved))
     solved.append(block)
-    return last_update(first, pivots, running, panels, solved, len(TREES))
+    return last_update(first, pivots, running, panel, solved, RANKS)
 
 
 def complex_dot(matrix, vectors):
@@ -312,13 +306,13 @@
     me = lax.axis_index("rows")
     per_device = right_sides.shape[1] // inverses.shape[-1]
     first = (me * per_device).reshape(1)
-    if ranks == len(TREES):
+    if ranks == RANKS:
         rows = solve_eight(first, right_sides, panels, inverses, pivots)
     else:
         owners = lax.div(pivots, jnp.full_like(pivots, per_device))
         solved = solve_summed(me, owners, right_sides, panels, inverses, pivots)
-        running = early_update(right_sides, panels, solved[:-1])
-        rows = last_update(first, pivots, running, panels, solved, ranks)
+        running, panel = early_update(right_sides, panels, solved[:-1])
+        rows = last_update(first, pivots, running, panel, solved, ranks)
     received = lax.all_to_all(rows, "rows", split_axis=0, concat_axis=0, tiled=True)
     return regroup(received)
 

time: 99.1 us -> 93.4 us (0.942)
  waiting for transfers between devices: 33.2 us -> 26.8 us
  Pallas kernels: 16.9 us -> 18.8 us
    ppermute x16, waiting for transfers between devices: 33.2 us -> 26.8 us  [the longest x4 9.48 us: run(): lax.ppermute(have, 'rows', sorted(((device, device ^ 2) for device in cor...]
    pallas_call x2 -> x4, Pallas kernels: 7.78 us -> 10.7 us  [the longest x3 5.55 us: prepare(): pl.pallas_call(functools.partial(prepare_kernel, numbers), out_shape=[jax...]
    pallas_call x1, Pallas kernels: 3.88 us -> 2.84 us  [last_update(): pl.pallas_call(functools.partial(last_kernel, owners), out_shape=jax.Shap...]
  transfers between devices with their start and end apart: 16 -> 16, of which waited for: 5 -> 8; matrix products, arithmetic and copies ran while one was open for 0% -> 0% of each run, Pallas kernels for 8% -> 12%
where the time goes in v1:
time: 93.4 us; the launch traced here: 92.3 us
  waiting for transfers between devices  26.8 us (29%)
  blocking collectives  22.1 us (24%)
  starting transfers between devices  21 us (22%)
  Pallas kernels  18.8 us (20%)
  between operations  2.76 us (3%)
    all_to_all x1, blocking collectives, body(): lax.all_to_all(rows, 'rows', split_axis=0, concat_axis=0, tiled=True)  22.1 us
    ppermute x8, starting transfers between devices, run(): lax.ppermute(value, 'rows', [(source, source ^ step)])  11.9 us
    ppermute x4, waiting for transfers between devices, run(): lax.ppermute(have, 'rows', sorted(((device, device ^ 2) for device in cor...  9.48 us
    ppermute x4, waiting for transfers between devices, run(): lax.ppermute(have, 'rows', [(source ^ 4, source ^ 5), (source, source ^ 7)])  9.07 us
    ppermute x8, waiting for transfers between devices, run(): lax.ppermute(value, 'rows', [(source, source ^ step)])  8.28 us
    pallas_call x3, Pallas kernels, prepare(): pl.pallas_call(functools.partial(prepare_kernel, numbers), out_shape=[jax...  5.55 us
    pallas_call x1, Pallas kernels, early_update(): pl.pallas_call(early_kernel, out_shape=[jax.ShapeDtypeStruct((height, loc...  5.19 us
    ppermute x4, starting transfers between devices, run(): lax.ppermute(have, 'rows', sorted(((device, device ^ 2) for device in cor...  5.18 us
  transfers between devices with their start and end apart: 16, of which 8 were waited for; matrix products, arithmetic and copies ran while one was open for 0% of the time, Pallas kernels for 12%

profile of v1, /device:TPU:0, one launch (start us, length us, event | category | flops | bytes accessed | tf_op | source)
XLA Modules:
  0.0 92.3 jit_solution(16260456306473572505)
XLA Ops:
  0.0 2.4 %solve_first.1 = (bf16[256,256]{1,0:T(8,128)(2,1)S(1)}, s32[1]{0:T(128)}, s32[1]{0:T(128)}, s32[1]{0:T(128)}, s32[1]{0:T(128)}) custom-call(s32[4]{0:T(128)} %pivots_ref.3, bf16[2,2048,128]{2,1,0:T(8,128)(2,1)} %sides_ref.1, bf16[4,2,256,256]{3,2,1,0:T(8,128)(2,1)} %inverse_ref.1), custom_call_target="tpu_custom_call" | custom-call | tf_op jit(solution)/shard_map/solve_first/pallas_call | solution.py:47
  3.0 16.3 %conditional.4 = (bf16[256,256]{1,0:T(8,128)(2,1)S(1)}, bf16[1280,256]{1,0:T(8,128)(2,1)S(1)}) conditional(s32[]{:T(128)} %bitcast.4, (s32[]{:T(128)}, bf16[256,256]{1,0:T(8,128)(2,1)S(1)}, s32[4]{0:T(128)S(1)}, bf16[4,2,256,256]{3,2,1,0:T(8,128)(2,1)S(1)}, bf16[2,2048,128]{2,1,0:T(8,128)(2,1)S(1)}, ...), branch_computations={%region_0.1_spmd, %region_1.2_spmd, %region_2.3_spmd, %region_3.4_... | conditional | flops 262145 | bytes 3145914 | solution.py:261
  3.1 6.0 %collective-permute-start = (bf16[256,256]{1,0:T(8,128)(2,1)S(1)}, bf16[256,256]{1,0:T(8,128)(2,1)S(1)}, u32[]{:S(2)}, u32[]{:S(2)}) collective-permute-start(bf16[256,256]{1,0:T(8,128)(2,1)S(1)} %get-tuple-element.406), channel_id=1, source_target_pairs={{0,8},{1,9},{16,24},{17,25}} | collective-permute-start | bytes 393224 | tf_op jit(solution)/shard_map/cond/branch_0_fun/ppermute | solution.py:251
  9.0 1.3 %collective-permute-start.1 = (bf16[256,256]{1,0:T(8,128)(2,1)S(1)}, bf16[256,256]{1,0:T(8,128)(2,1)S(1)}, u32[]{:S(2)}, u32[]{:S(2)}) collective-permute-start(bf16[256,256]{1,0:T(8,128)(2,1)S(1)} %get-tuple-element.406), channel_id=1, source_target_pairs={{0,2},{1,3},{16,18},{17,19}} | collective-permute-start | bytes 393224 | tf_op jit(solution)/shard_map/cond/branch_0_fun/ppermute | solution.py:251
  10.3 1.4 %collective-permute-done = bf16[256,256]{1,0:T(8,128)(2,1)S(1)} collective-permute-done((bf16[256,256]{1,0:T(8,128)(2,1)S(1)}, bf16[256,256]{1,0:T(8,128)(2,1)S(1)}, u32[]{:S(2)}, u32[]{:S(2)}) %collective-permute-start) | collective-permute-done | bytes 131104 | tf_op jit(solution)/shard_map/cond/branch_0_fun/ppermute | solution.py:251
  11.8 1.3 %collective-permute-done.1 = bf16[256,256]{1,0:T(8,128)(2,1)S(1)} collective-permute-done((bf16[256,256]{1,0:T(8,128)(2,1)S(1)}, bf16[256,256]{1,0:T(8,128)(2,1)S(1)}, u32[]{:S(2)}, u32[]{:S(2)}) %collective-permute-start.1) | collective-permute-done | bytes 131104 | tf_op jit(solution)/shard_map/cond/branch_0_fun/ppermute | solution.py:251
  13.1 1.3 %collective-permute-start.2 = (bf16[256,256]{1,0:T(8,128)(2,1)S(1)}, bf16[256,256]{1,0:T(8,128)(2,1)S(1)}, u32[]{:S(2)}, u32[]{:S(2)}) collective-permute-start(bf16[256,256]{1,0:T(8,128)(2,1)S(1)} %add_select_fusion), channel_id=1, source_target_pairs={{0,4},{2,6},{8,12},{10,14},{1,5},{3,7},{9,13},{11,15},{16,20},{18,... | collective-permute-start | bytes 393224 | tf_op jit(solution)/shard_map/cond/branch_0_fun/ppermute | solution.py:255
  14.4 1.3 %collective-permute-start.3 = (bf16[256,256]{1,0:T(8,128)(2,1)S(1)}, bf16[256,256]{1,0:T(8,128)(2,1)S(1)}, u32[]{:S(2)}, u32[]{:S(2)}) collective-permute-start(bf16[256,256]{1,0:T(8,128)(2,1)S(1)} %add_select_fusion), channel_id=1, source_target_pairs={{8,10},{0,14},{9,11},{1,15},{24,26},{16,30},{25,27},{17,31}} | collective-permute-start | bytes 393224 | tf_op jit(solution)/shard_map/cond/branch_0_fun/ppermute | solution.py:256
  15.7 1.7 %prepare.24 = bf16[1280,256]{1,0:T(8,128)(2,1)S(1)} custom-call(s32[4]{0:T(128)S(1)} %get-tuple-element.407.pivots_ref, bf16[4,2,256,256]{3,2,1,0:T(8,128)(2,1)S(1)} %get-tuple-element.408.inverse_ref, bf16[2,2048,128]{2,1,0:T(8,128)(2,1)S(1)} %get-tuple-element.409.refs_0_, bf16[2,2048,1024]{2,1,0:T(8,128)(2,1)} %get-tuple-element.410.refs_1_), custom_call_target="tpu_custom_call" | custom-call | tf_op jit(solution)/shard_map/cond/branch_0_fun/prepare/pallas_call | solution.py:90
  17.9 1.4 %collective-permute-done.3 = bf16[256,256]{1,0:T(8,128)(2,1)S(1)} collective-permute-done((bf16[256,256]{1,0:T(8,128)(2,1)S(1)}, bf16[256,256]{1,0:T(8,128)(2,1)S(1)}, u32[]{:S(2)}, u32[]{:S(2)}) %collective-permute-start.3) | collective-permute-done | bytes 131104 | tf_op jit(solution)/shard_map/cond/branch_0_fun/ppermute | solution.py:256
  20.6 16.0 %conditional.5 = (bf16[256,256]{1,0:T(8,128)(2,1)S(1)}, bf16[1792,256]{1,0:T(8,128)(2,1)S(1)}) conditional(s32[]{:T(128)} %bitcast.3, (s32[]{:T(128)}, bf16[256,256]{1,0:T(8,128)(2,1)S(1)}, s32[4]{0:T(128)S(1)}, bf16[4,2,256,256]{3,2,1,0:T(8,128)(2,1)S(1)}, bf16[2,2048,128]{2,1,0:T(8,128)(2,1)S(1)}, ...), branch_computations={%region_8.9_spmd, %region_9.10_spmd, %region_10.11_spmd, %region_1... | conditional | flops 262145 | bytes 3145914 | solution.py:261
  22.0 1.3 %collective-permute-start.62 = (bf16[256,256]{1,0:T(8,128)(2,1)S(1)}, bf16[256,256]{1,0:T(8,128)(2,1)S(1)}, u32[]{:S(2)}, u32[]{:S(2)}) collective-permute-start(bf16[256,256]{1,0:T(8,128)(2,1)S(1)} %add_select_fusion.15), channel_id=1, source_target_pairs={{4,0},{6,2},{12,8},{14,10},{5,1},{7,3},{13,9},{15,11},{20,16},{22,... | collective-permute-start | bytes 393224 | tf_op jit(solution)/shard_map/cond/branch_7_fun/ppermute | solution.py:255
  24.6 1.9 %prepare.39 = bf16[1792,256]{1,0:T(8,128)(2,1)S(1)} custom-call(s32[4]{0:T(128)S(1)} %get-tuple-element.497.pivots_ref, bf16[4,2,256,256]{3,2,1,0:T(8,128)(2,1)S(1)} %get-tuple-element.498.inverse_ref, bf16[2,2048,128]{2,1,0:T(8,128)(2,1)S(1)} %get-tuple-element.499.refs_0_, bf16[2,2048,1024]{2,1,0:T(8,128)(2,1)} %get-tuple-element.500.refs_1_), custom_call_target="tpu_custom_call" | custom-call | tf_op jit(solution)/shard_map/cond/branch_7_fun/prepare/pallas_call | solution.py:90
  26.5 2.4 %collective-permute-done.62 = bf16[256,256]{1,0:T(8,128)(2,1)S(1)} collective-permute-done((bf16[256,256]{1,0:T(8,128)(2,1)S(1)}, bf16[256,256]{1,0:T(8,128)(2,1)S(1)}, u32[]{:S(2)}, u32[]{:S(2)}) %collective-permute-start.62) | collective-permute-done | bytes 131104 | tf_op jit(solution)/shard_map/cond/branch_7_fun/ppermute | solution.py:255
  28.9 7.7 %collective-permute-done.63 = bf16[256,256]{1,0:T(8,128)(2,1)S(1)} collective-permute-done((bf16[256,256]{1,0:T(8,128)(2,1)S(1)}, bf16[256,256]{1,0:T(8,128)(2,1)S(1)}, u32[]{:S(2)}, u32[]{:S(2)}) %collective-permute-start.63) | collective-permute-done | bytes 131104 | tf_op jit(solution)/shard_map/cond/branch_7_fun/ppermute | solution.py:256
  37.8 12.2 %conditional.6 = (bf16[256,256]{1,0:T(8,128)(2,1)S(1)}, bf16[2304,256]{1,0:T(8,128)(2,1)S(1)}) conditional(s32[]{:T(128)} %bitcast.2, (s32[]{:T(128)}, bf16[256,256]{1,0:T(8,128)(2,1)S(1)}, s32[4]{0:T(128)S(1)}, bf16[4,2,256,256]{3,2,1,0:T(8,128)(2,1)S(1)}, bf16[2,2048,128]{2,1,0:T(8,128)(2,1)S(1)}, ...), branch_computations={%region_16.17_spmd, %region_17.18_spmd, %region_18.19_spmd, %regio... | conditional | flops 262145 | bytes 3145914 | solution.py:261
  41.2 2.0 %prepare.43 = bf16[2304,256]{1,0:T(8,128)(2,1)S(1)} custom-call(s32[4]{0:T(128)S(1)} %get-tuple-element.521.pivots_ref, bf16[4,2,256,256]{3,2,1,0:T(8,128)(2,1)S(1)} %get-tuple-element.522.inverse_ref, bf16[2,2048,128]{2,1,0:T(8,128)(2,1)S(1)} %get-tuple-element.523.refs_0_, bf16[2,2048,1024]{2,1,0:T(8,128)(2,1)} %get-tuple-element.524.refs_1_), custom_call_target="tpu_custom_call" | custom-call | tf_op jit(solution)/shard_map/cond/branch_3_fun/prepare/pallas_call | solution.py:90
  43.2 6.6 %collective-permute-done.78 = bf16[256,256]{1,0:T(8,128)(2,1)S(1)} collective-permute-done((bf16[256,256]{1,0:T(8,128)(2,1)S(1)}, bf16[256,256]{1,0:T(8,128)(2,1)S(1)}, u32[]{:S(2)}, u32[]{:S(2)}) %collective-permute-start.78) | collective-permute-done | bytes 131104 | tf_op jit(solution)/shard_map/cond/branch_3_fun/ppermute | solution.py:255
  51.3 14.8 %conditional.7 = (bf16[256,256]{1,0:T(8,128)(2,1)S(1)}, f32[256,2048]{1,0:T(8,128)S(1)}, bf16[2,2048,256]{2,1,0:T(8,128)(2,1)S(1)}) conditional(s32[]{:T(128)} %bitcast.1, (s32[]{:T(128)}, bf16[256,256]{1,0:T(8,128)(2,1)S(1)}, bf16[2,2048,128]{2,1,0:T(8,128)(2,1)S(1)}, bf16[2,2048,1024]{2,1,0:T(8,128)(2,1)}, ...), branch_computations={%region_24.25_spmd, %region_25.26_spmd, %region_26.27_spmd, %regio... | conditional | flops 262145 | bytes 3145922 | solution.py:261
  53.4 5.5 %collective-permute-done.101 = bf16[256,256]{1,0:T(8,128)(2,1)S(1)} collective-permute-done((bf16[256,256]{1,0:T(8,128)(2,1)S(1)}, bf16[256,256]{1,0:T(8,128)(2,1)S(1)}, u32[]{:S(2)}, u32[]{:S(2)}) %collective-permute-start.101) | collective-permute-done | bytes 131104 | tf_op jit(solution)/shard_map/cond/branch_1_fun/ppermute | solution.py:251
  58.9 1.3 %collective-permute-start.102 = (bf16[256,256]{1,0:T(8,128)(2,1)S(1)}, bf16[256,256]{1,0:T(8,128)(2,1)S(1)}, u32[]{:S(2)}, u32[]{:S(2)}) collective-permute-start(bf16[256,256]{1,0:T(8,128)(2,1)S(1)} %add_select_fusion.25), channel_id=1, source_target_pairs={{0,4},{2,6},{8,12},{10,14},{1,5},{3,7},{9,13},{11,15},{16,20},{18,... | collective-permute-start | bytes 393224 | tf_op jit(solution)/shard_map/cond/branch_1_fun/ppermute | solution.py:255
  60.9 5.2 %early_update.9 = (f32[256,2048]{1,0:T(8,128)S(1)}, bf16[2,2048,256]{2,1,0:T(8,128)(2,1)S(1)}) custom-call(bf16[2,2048,128]{2,1,0:T(8,128)(2,1)S(1)} %get-tuple-element.560.sides_ref, bf16[2,2048,1024]{2,1,0:T(8,128)(2,1)} %get-tuple-element.561.panel_ref, bf16[256,256]{1,0:T(8,128)(2,1)S(1)} %get-tuple-element.562.refs_0_, ...), custom_call_target="tpu_custom_call" | custom-call | tf_op jit(solution)/shard_map/cond/branch_1_fun/early_update/pallas_call | solution.py:158
  66.2 2.8 %last_update.1 = bf16[8,2,16,2048]{3,2,1,0:T(8,128)(2,1)S(1)} custom-call(s32[4]{0:T(128)S(1)} %copy-done.2, s32[1]{0:T(128)} %bitcast.first_ref, f32[256,2048]{1,0:T(8,128)S(1)} %get-tuple-element.646.running_ref, bf16[2,2048,256]{2,1,0:T(8,128)(2,1)S(1)} %get-tuple-element.647.panel_ref, bf16[256,256]{1,0:T(8,128)(2,1)S(1)} %get-tuple-element.641.refs_0_, ...), custom_call_target="tpu_custom_call" | custom-call | tf_op jit(solution)/shard_map/last_update/pallas_call | solution.py:210
  69.0 22.1 %all_to_all.5.rows_ref = bf16[8,2,16,2048]{3,2,1,0:T(8,128)(2,1)S(1)} all-to-all(bf16[8,2,16,2048]{3,2,1,0:T(8,128)(2,1)S(1)} %last_update.1), channel_id=1, replica_groups=mesh['groups'=2,'rows'=8,'shots'=2] {'rows'}, dimensions={0} | all-to-all | bytes 2097152 | tf_op jit(solution)/shard_map/all_to_all | solution.py:316
  (37 shorter events, 12.1 us)
Async XLA Ops:
  0.0 3.0 %copy-start = (bf16[2,2048,128]{2,1,0:T(8,128)(2,1)S(1)}, bf16[2,2048,128]{2,1,0:T(8,128)(2,1)}, u32[]{:S(2)}) copy-start(bf16[2,2048,128]{2,1,0:T(8,128)(2,1)} %sides_ref.1) | copy-start | bytes 3145732
  0.0 3.0 %copy-start.1 = (bf16[4,2,256,256]{3,2,1,0:T(8,128)(2,1)S(1)}, bf16[4,2,256,256]{3,2,1,0:T(8,128)(2,1)}, u32[]{:S(2)}) copy-start(bf16[4,2,256,256]{3,2,1,0:T(8,128)(2,1)} %inverse_ref.1) | copy-start | bytes 3145732
  0.0 3.0 %copy-start.2 = (s32[4]{0:T(128)S(1)}, s32[4]{0:T(128)}, u32[]{:S(2)}) copy-start(s32[4]{0:T(128)} %pivots_ref.3) | copy-start | bytes 52
  3.1 8.7 %collective-permute-start = (bf16[256,256]{1,0:T(8,128)(2,1)S(1)}, bf16[256,256]{1,0:T(8,128)(2,1)S(1)}, u32[]{:S(2)}, u32[]{:S(2)}) collective-permute-start(bf16[256,256]{1,0:T(8,128)(2,1)S(1)} %get-tuple-element.406), channel_id=1, source_target_pairs={{0,8},{1,9},{16,24},{17,25}} | collective-permute-start | bytes 393224 | tf_op jit(solution)/shard_map/cond/branch_0_fun/ppermute | solution.py:251
  9.0 4.0 %collective-permute-start.1 = (bf16[256,256]{1,0:T(8,128)(2,1)S(1)}, bf16[256,256]{1,0:T(8,128)(2,1)S(1)}, u32[]{:S(2)}, u32[]{:S(2)}) collective-permute-start(bf16[256,256]{1,0:T(8,128)(2,1)S(1)} %get-tuple-element.406), channel_id=1, source_target_pairs={{0,2},{1,3},{16,18},{17,19}} | collective-permute-start | bytes 393224 | tf_op jit(solution)/shard_map/cond/branch_0_fun/ppermute | solution.py:251
  13.1 4.8 %collective-permute-start.2 = (bf16[256,256]{1,0:T(8,128)(2,1)S(1)}, bf16[256,256]{1,0:T(8,128)(2,1)S(1)}, u32[]{:S(2)}, u32[]{:S(2)}) collective-permute-start(bf16[256,256]{1,0:T(8,128)(2,1)S(1)} %add_select_fusion), channel_id=1, source_target_pairs={{0,4},{2,6},{8,12},{10,14},{1,5},{3,7},{9,13},{11,15},{16,20},{18,... | collective-permute-start | bytes 393224 | tf_op jit(solution)/shard_map/cond/branch_0_fun/ppermute | solution.py:255
  14.4 4.9 %collective-permute-start.3 = (bf16[256,256]{1,0:T(8,128)(2,1)S(1)}, bf16[256,256]{1,0:T(8,128)(2,1)S(1)}, u32[]{:S(2)}, u32[]{:S(2)}) collective-permute-start(bf16[256,256]{1,0:T(8,128)(2,1)S(1)} %add_select_fusion), channel_id=1, source_target_pairs={{8,10},{0,14},{9,11},{1,15},{24,26},{16,30},{25,27},{17,31}} | collective-permute-start | bytes 393224 | tf_op jit(solution)/shard_map/cond/branch_0_fun/ppermute | solution.py:256
  20.6 1.4 %collective-permute-start.60 = (bf16[256,256]{1,0:T(8,128)(2,1)S(1)}, bf16[256,256]{1,0:T(8,128)(2,1)S(1)}, u32[]{:S(2)}, u32[]{:S(2)}) collective-permute-start(bf16[256,256]{1,0:T(8,128)(2,1)S(1)} %get-tuple-element.496), channel_id=1, source_target_pairs={{14,6},{15,7},{30,22},{31,23}} | collective-permute-start | bytes 393224 | tf_op jit(solution)/shard_map/cond/branch_7_fun/ppermute | solution.py:251
  21.3 0.7 collective-permute-start.61
  22.0 6.9 %collective-permute-start.62 = (bf16[256,256]{1,0:T(8,128)(2,1)S(1)}, bf16[256,256]{1,0:T(8,128)(2,1)S(1)}, u32[]{:S(2)}, u32[]{:S(2)}) collective-permute-start(bf16[256,256]{1,0:T(8,128)(2,1)S(1)} %add_select_fusion.15), channel_id=1, source_target_pairs={{4,0},{6,2},{12,8},{14,10},{5,1},{7,3},{13,9},{15,11},{20,16},{22,... | collective-permute-start | bytes 393224 | tf_op jit(solution)/shard_map/cond/branch_7_fun/ppermute | solution.py:255
  23.3 13.2 %collective-permute-start.63 = (bf16[256,256]{1,0:T(8,128)(2,1)S(1)}, bf16[256,256]{1,0:T(8,128)(2,1)S(1)}, u32[]{:S(2)}, u32[]{:S(2)}) collective-permute-start(bf16[256,256]{1,0:T(8,128)(2,1)S(1)} %add_select_fusion.15), channel_id=1, source_target_pairs={{6,4},{14,0},{7,5},{15,1},{22,20},{30,16},{23,21},{31,17}} | collective-permute-start | bytes 393224 | tf_op jit(solution)/shard_map/cond/branch_7_fun/ppermute | solution.py:256
  37.8 1.4 %collective-permute-start.76 = (bf16[256,256]{1,0:T(8,128)(2,1)S(1)}, bf16[256,256]{1,0:T(8,128)(2,1)S(1)}, u32[]{:S(2)}, u32[]{:S(2)}) collective-permute-start(bf16[256,256]{1,0:T(8,128)(2,1)S(1)} %get-tuple-element.520), channel_id=1, source_target_pairs={{6,14},{7,15},{22,30},{23,31}} | collective-permute-start | bytes 393224 | tf_op jit(solution)/shard_map/cond/branch_3_fun/ppermute | solution.py:251
  38.5 0.7 collective-permute-start.77
  39.2 10.5 %collective-permute-start.78 = (bf16[256,256]{1,0:T(8,128)(2,1)S(1)}, bf16[256,256]{1,0:T(8,128)(2,1)S(1)}, u32[]{:S(2)}, u32[]{:S(2)}) collective-permute-start(bf16[256,256]{1,0:T(8,128)(2,1)S(1)} %add_select_fusion.19), channel_id=1, source_target_pairs={{4,0},{6,2},{12,8},{14,10},{5,1},{7,3},{13,9},{15,11},{20,16},{22,... | collective-permute-start | bytes 393224 | tf_op jit(solution)/shard_map/cond/branch_3_fun/ppermute | solution.py:255
  40.5 9.2 %collective-permute-start.79 = (bf16[256,256]{1,0:T(8,128)(2,1)S(1)}, bf16[256,256]{1,0:T(8,128)(2,1)S(1)}, u32[]{:S(2)}, u32[]{:S(2)}) collective-permute-start(bf16[256,256]{1,0:T(8,128)(2,1)S(1)} %add_select_fusion.19), channel_id=1, source_target_pairs={{14,12},{6,8},{15,13},{7,9},{30,28},{22,24},{31,29},{23,25}} | collective-permute-start | bytes 393224 | tf_op jit(solution)/shard_map/cond/branch_3_fun/ppermute | solution.py:256
  51.4 2.0 %collective-permute-start.100 = (bf16[256,256]{1,0:T(8,128)(2,1)S(1)}, bf16[256,256]{1,0:T(8,128)(2,1)S(1)}, u32[]{:S(2)}, u32[]{:S(2)}) collective-permute-start(bf16[256,256]{1,0:T(8,128)(2,1)S(1)} %get-tuple-element.559), channel_id=1, source_target_pairs={{2,10},{3,11},{18,26},{19,27}} | collective-permute-start | bytes 393224 | tf_op jit(solution)/shard_map/cond/branch_1_fun/ppermute | solution.py:251
  52.0 6.9 %collective-permute-start.101 = (bf16[256,256]{1,0:T(8,128)(2,1)S(1)}, bf16[256,256]{1,0:T(8,128)(2,1)S(1)}, u32[]{:S(2)}, u32[]{:S(2)}) collective-permute-start(bf16[256,256]{1,0:T(8,128)(2,1)S(1)} %get-tuple-element.559), channel_id=1, source_target_pairs={{2,0},{3,1},{18,16},{19,17}} | collective-permute-start | bytes 393224 | tf_op jit(solution)/shard_map/cond/branch_1_fun/ppermute | solution.py:251
  58.9 7.2 %collective-permute-start.102 = (bf16[256,256]{1,0:T(8,128)(2,1)S(1)}, bf16[256,256]{1,0:T(8,128)(2,1)S(1)}, u32[]{:S(2)}, u32[]{:S(2)}) collective-permute-start(bf16[256,256]{1,0:T(8,128)(2,1)S(1)} %add_select_fusion.25), channel_id=1, source_target_pairs={{0,4},{2,6},{8,12},{10,14},{1,5},{3,7},{9,13},{11,15},{16,20},{18,... | collective-permute-start | bytes 393224 | tf_op jit(solution)/shard_map/cond/branch_1_fun/ppermute | solution.py:255
  60.2 5.9 %collective-permute-start.103 = (bf16[256,256]{1,0:T(8,128)(2,1)S(1)}, bf16[256,256]{1,0:T(8,128)(2,1)S(1)}, u32[]{:S(2)}, u32[]{:S(2)}) collective-permute-start(bf16[256,256]{1,0:T(8,128)(2,1)S(1)} %add_select_fusion.25), channel_id=1, source_target_pairs={{10,8},{2,12},{11,9},{3,13},{26,24},{18,28},{27,25},{19,29}} | collective-permute-start | bytes 393224 | tf_op jit(solution)/shard_map/cond/branch_1_fun/ppermute | solution.py:256

commit v2 on v1

--- a/solution.py
+++ b/solution.py
@@ -177,70 +177,76 @@
     )(right_sides, panels, *solved)
 
 
-def last_kernel(owners, pivots_ref, first_ref, running_ref, panel_ref, *refs):
-    solved_refs, out_ref = refs[:-1], refs[-1]
+def last_kernel(panels, pivots_ref, me_ref, running_ref, panel_ref, *refs):
+    width = panel_ref.shape[2]
     height, rows = running_ref.shape
-    width = solved_refs[0].shape[1]
-    shots = height // 2
-    each = shots // owners
-
-    def write(values, k):
-        for part in range(2):
-            for owner in range(owners):
-                start = part * shots + owner * each
-                out_ref[owner, part, :, k * width : (k + 1) * width] = values[start : start + each]
-
+    solved_refs, out_refs, whole_ref = refs[:panels], refs[panels:-1], refs[-1]
+    count = len(out_refs)
     solved = solved_refs[-1][...]
     around = turned(solved)
+    first = me_ref[0] * (rows // width)
     for k in range(rows // width):
         columns = slice(k * width, (k + 1) * width)
         values = running_ref[:, columns] - dot_t(solved, panel_ref[0, columns])
-        write((values - dot_t(around, panel_ref[1, columns])).astype(jnp.bfloat16), k)
-        for j, solved_ref in enumerate(solved_refs):
-
-            @pl.when(pivots_ref[j] == first_ref[0] + k)
+        whole_ref[:, columns] = (values - dot_t(around, panel_ref[1, columns])).astype(jnp.bfloat16)
+    for j, solved_ref in enumerate(solved_refs):
+        for k in range(rows // width):
+
+            @pl.when(pivots_ref[j] == first + k)
             def _():
-                write(solved_ref[...], k)
-
-
-def last_update(first, pivots, running, panel, solved, owners):
+                whole_ref[:, k * width : (k + 1) * width] = solved_ref[...]
+
+    each = height // 2 // count
+    for step, out_ref in enumerate(out_refs):
+        for part in range(2):
+            start = pl.multiple_of((part * count + (me_ref[0] ^ step)) * each, each)
+            out_ref[part] = whole_ref[pl.ds(start, each), :]
+
+
+def last_update(me, pivots, running, panel, solved, owners):
     parts, local_rows, _ = panel.shape
     height, width = solved[0].shape
     each = height // parts // owners
     return pl.pallas_call(
-        functools.partial(last_kernel, owners),
-        out_shape=jax.ShapeDtypeStruct((owners, parts, each, local_rows), jnp.bfloat16),
+        functools.partial(last_kernel, len(solved)),
+        out_shape=[jax.ShapeDtypeStruct((parts, each, local_rows), jnp.bfloat16)] * owners,
         in_specs=[pl.BlockSpec(memory_space=pltpu.SMEM)] * 2
         + [pl.BlockSpec(memory_space=pltpu.VMEM)] * (2 + len(solved)),
-        out_specs=pl.BlockSpec(memory_space=pltpu.VMEM),
+        out_specs=[pl.BlockSpec(memory_space=pltpu.VMEM)] * owners,
+        scratch_shapes=[pltpu.VMEM((height, local_rows), jnp.bfloat16)],
         compiler_params=SMALL,
         name="last_update",
-    )(pivots, first, running, panel, *solved)
-
-
-def regroup_kernel(rows_ref, out_ref, sems):
-    owners, _, _, rows = rows_ref.shape
-    copies = [
-        pltpu.make_async_copy(rows_ref.at[owner], out_ref.at[:, 0, :, pl.ds(owner * rows, rows)], sems.at[owner])
-        for owner in range(owners)
-    ]
+    )(pivots, me, running, panel, *solved)
+
+
+def regroup_kernel(me_ref, *refs):
+    block_refs, out_ref, sems = refs[:-2], refs[-2], refs[-1]
+    rows = block_refs[0].shape[2]
+    copies = []
+    for step, block_ref in enumerate(block_refs):
+        start = pl.multiple_of((me_ref[0] ^ step) * rows, rows)
+        copies.append(pltpu.make_async_copy(block_ref, out_ref.at[:, 0, :, pl.ds(start, rows)], sems.at[step]))
     for copy in copies:
         copy.start()
     for copy in copies:
         copy.wait()
 
 
-def regroup(received):
-    owners, parts, shots, rows = received.shape
+def regroup(me, blocks):
+    parts, shots, rows = blocks[0].shape
     return pl.pallas_call(
         regroup_kernel,
-        out_shape=jax.ShapeDtypeStruct((parts, 1, shots, owners * rows), received.dtype),
-        in_specs=[pl.BlockSpec(memory_space=pltpu.VMEM)],
-        out_specs=pl.BlockSpec(memory_space=pl.ANY),
-        scratch_shapes=[pltpu.SemaphoreType.DMA((owners,))],
+        out_shape=jax.ShapeDtypeStruct((parts, 1, shots, len(blocks) * rows), blocks[0].dtype),
+        grid_spec=pltpu.PrefetchScalarGridSpec(
+            num_scalar_prefetch=1,
+            grid=(1,),
+            in_specs=[pl.BlockSpec(memory_space=pltpu.VMEM)] * len(blocks),
+            out_specs=pl.BlockSpec(memory_space=pl.ANY),
+            scratch_shapes=[pltpu.SemaphoreType.DMA((len(blocks),))],
+        ),
         compiler_params=SMALL,
         name="regroup",
-    )(received)
+    )(me, *blocks)
 
 
 def broadcast(block, owner, beside):
@@ -248,12 +254,12 @@
 
     def branch(source):
         def run(value):
-            early = [lax.ppermute(value, "rows", [(source, source ^ step)]) for step in (4, 1)]
+            early = [lax.ppermute(value, "rows", [(source, source ^ step)]) for step in (1, 4)]
             have = jnp.where(me == source, value, early[0] + early[1])
             results = beside()
             corner = [source ^ step for step in (0, 1, 4, 5)]
+            fourth = lax.ppermute(have, "rows", [(source ^ 4, source ^ 5), (source, source ^ 7)])
             third = lax.ppermute(have, "rows", sorted((device, device ^ 2) for device in corner))
-            fourth = lax.ppermute(have, "rows", [(source ^ 4, source ^ 5), (source, source ^ 7)])
             return have + third + fourth, results
 
         return run
@@ -261,7 +267,7 @@
     return lax.switch(owner, [branch(source) for source in range(RANKS)], block)
 
 
-def solve_eight(first, right_sides, panels, inverses, pivots):
+def solve_eight(right_sides, panels, inverses, pivots):
     last = inverses.shape[0] - 1
     block, *owners = solve_first(pivots, right_sides, inverses)
     owners = [owner[0] for owner in owners]
@@ -277,7 +283,7 @@
     block = solve(own[last - 1], solved)
     block, (running, panel) = broadcast(block, owners[last], lambda: early_update(right_sides, panels, solved))
     solved.append(block)
-    return last_update(first, pivots, running, panel, solved, RANKS)
+    return solved, running, panel
 
 
 def complex_dot(matrix, vectors):
@@ -304,17 +310,18 @@
 
 def body(ranks, right_sides, panels, inverses, pivots):
     me = lax.axis_index("rows")
-    per_device = right_sides.shape[1] // inverses.shape[-1]
-    first = (me * per_device).reshape(1)
     if ranks == RANKS:
-        rows = solve_eight(first, right_sides, panels, inverses, pivots)
+        solved, running, panel = solve_eight(right_sides, panels, inverses, pivots)
     else:
+        per_device = right_sides.shape[1] // inverses.shape[-1]
         owners = lax.div(pivots, jnp.full_like(pivots, per_device))
         solved = solve_summed(me, owners, right_sides, panels, inverses, pivots)
         running, panel = early_update(right_sides, panels, solved[:-1])
-        rows = last_update(first, pivots, running, panel, solved, ranks)
-    received = lax.all_to_all(rows, "rows", split_axis=0, concat_axis=0, tiled=True)
-    return regroup(received)
+    me = me.reshape(1)
+    blocks = list(last_update(me, pivots, running, panel, solved, ranks))
+    for step in range(1, ranks):
+        blocks[step] = lax.ppermute(blocks[step], "rows", [(i, i ^ step) for i in range(ranks)])
+    return regroup(me, blocks)
 
 
 def solution(mesh):

time: 93.4 us -> 92.4 us (0.989)
  blocking collectives: 22.1 us -> 0 us
  waiting for transfers between devices: 26.8 us -> 37.7 us
  starting transfers between devices: 21 us -> 31.9 us
  Pallas kernels: 18.8 us -> 17.6 us
    all_to_all x1 -> x0, blocking collectives: 22.1 us -> none  [body(): lax.all_to_all(rows, 'rows', split_axis=0, concat_axis=0, tiled=True)]
    ppermute x0 -> x7, starting transfers between devices: none -> 12.4 us  [body(): lax.ppermute(blocks[step], 'rows', [(i, i ^ step) for i in range(ranks)])]
    ppermute x4, waiting for transfers between devices: 9.07 us -> 19.7 us  [run(): lax.ppermute(have, 'rows', [(source ^ 4, source ^ 5), (source, source ^ 7)])]
    ppermute x0 -> x7, waiting for transfers between devices: none -> 8.2 us  [body(): lax.ppermute(blocks[step], 'rows', [(i, i ^ step) for i in range(ranks)])]
    ppermute x8, waiting for transfers between devices: 8.28 us -> 2.51 us  [run(): lax.ppermute(value, 'rows', [(source, source ^ step)])]
    ppermute x4, waiting for transfers between devices: 9.48 us -> 7.33 us  [run(): lax.ppermute(have, 'rows', sorted(((device, device ^ 2) for device in cor...]
    ppermute x8, starting transfers between devices: 11.9 us -> 9.78 us  [run(): lax.ppermute(value, 'rows', [(source, source ^ step)])]
    pallas_call x1, Pallas kernels: 2.84 us -> 1.61 us  [last_update(): pl.pallas_call(functools.partial(last_kernel, len(solved)), out_shape=[ja...]
  transfers between devices with their start and end apart: 16 -> 23, of which waited for: 8 -> 7; matrix products, arithmetic and copies ran while one was open for 0% -> 0% of each run, Pallas kernels for 12% -> 12%
where the time goes in v2:
time: 92.4 us; the launch traced here: 90.8 us
  waiting for transfers between devices  37.7 us (41%)
  starting transfers between devices  31.9 us (35%)
  Pallas kernels  17.6 us (19%)
  between operations  2.77 us (3%)
    ppermute x4, waiting for transfers between devices, run(): lax.ppermute(have, 'rows', [(source ^ 4, source ^ 5), (source, source ^ 7)])  19.7 us
    ppermute x7, starting transfers between devices, body(): lax.ppermute(blocks[step], 'rows', [(i, i ^ step) for i in range(ranks)])  12.4 us
    ppermute x8, starting transfers between devices, run(): lax.ppermute(value, 'rows', [(source, source ^ step)])  9.78 us
    ppermute x7, waiting for transfers between devices, body(): lax.ppermute(blocks[step], 'rows', [(i, i ^ step) for i in range(ranks)])  8.2 us
    ppermute x4, waiting for transfers between devices, run(): lax.ppermute(have, 'rows', sorted(((device, device ^ 2) for device in cor...  7.33 us
    pallas_call x3, Pallas kernels, prepare(): pl.pallas_call(functools.partial(prepare_kernel, numbers), out_shape=[jax...  5.55 us
    pallas_call x1, Pallas kernels, early_update(): pl.pallas_call(early_kernel, out_shape=[jax.ShapeDtypeStruct((height, loc...  5.19 us
    ppermute x4, starting transfers between devices, run(): lax.ppermute(have, 'rows', sorted(((device, device ^ 2) for device in cor...  5.17 us
  transfers between devices with their start and end apart: 23, of which 7 were waited for; matrix products, arithmetic and copies ran while one was open for 0% of the time, Pallas kernels for 12%

profile of v2, /device:TPU:0, one launch (start us, length us, event | category | flops | bytes accessed | tf_op | source)
XLA Modules:
  0.0 90.8 jit_solution(2463376331165293807)
XLA Ops:
  0.0 2.4 %solve_first.1 = (bf16[256,256]{1,0:T(8,128)(2,1)S(1)}, s32[1]{0:T(128)}, s32[1]{0:T(128)}, s32[1]{0:T(128)}, s32[1]{0:T(128)}) custom-call(s32[4]{0:T(128)} %pivots_ref.3, bf16[2,2048,128]{2,1,0:T(8,128)(2,1)} %sides_ref.1, bf16[4,2,256,256]{3,2,1,0:T(8,128)(2,1)} %inverse_ref.1), custom_call_target="tpu_custom_call" | custom-call | tf_op jit(solution)/shard_map/solve_first/pallas_call | solution.py:47
  4.9 17.7 %conditional.4 = (bf16[256,256]{1,0:T(8,128)(2,1)S(1)}, bf16[1280,256]{1,0:T(8,128)(2,1)S(1)}) conditional(s32[]{:T(128)} %bitcast.4, (s32[]{:T(128)}, bf16[256,256]{1,0:T(8,128)(2,1)S(1)}, s32[4]{0:T(128)S(1)}, bf16[4,2,256,256]{3,2,1,0:T(8,128)(2,1)S(1)}, bf16[2,2048,128]{2,1,0:T(8,128)(2,1)S(1)}, ...), branch_computations={%region_0.1_spmd, %region_1.2_spmd, %region_2.3_spmd, %region_3.4_... | conditional | flops 262145 | bytes 3145914 | solution.py:267
  9.0 1.7 %prepare.31 = bf16[1280,256]{1,0:T(8,128)(2,1)S(1)} custom-call(s32[4]{0:T(128)S(1)} %get-tuple-element.449.pivots_ref, bf16[4,2,256,256]{3,2,1,0:T(8,128)(2,1)S(1)} %get-tuple-element.450.inverse_ref, bf16[2,2048,128]{2,1,0:T(8,128)(2,1)S(1)} %get-tuple-element.451.refs_0_, bf16[2,2048,1024]{2,1,0:T(8,128)(2,1)} %get-tuple-element.452.refs_1_), custom_call_target="tpu_custom_call" | custom-call | tf_op jit(solution)/shard_map/cond/branch_7_fun/prepare/pallas_call | solution.py:90
  10.7 11.9 %collective-permute-done.31 = bf16[256,256]{1,0:T(8,128)(2,1)S(1)} collective-permute-done((bf16[256,256]{1,0:T(8,128)(2,1)S(1)}, bf16[256,256]{1,0:T(8,128)(2,1)S(1)}, u32[]{:S(2)}, u32[]{:S(2)}) %collective-permute-start.31) | collective-permute-done | bytes 131104 | tf_op jit(solution)/shard_map/cond/branch_7_fun/ppermute | solution.py:261
  23.2 13.7 %conditional.5 = (bf16[256,256]{1,0:T(8,128)(2,1)S(1)}, bf16[1792,256]{1,0:T(8,128)(2,1)S(1)}) conditional(s32[]{:T(128)} %bitcast.3, (s32[]{:T(128)}, bf16[256,256]{1,0:T(8,128)(2,1)S(1)}, s32[4]{0:T(128)S(1)}, bf16[4,2,256,256]{3,2,1,0:T(8,128)(2,1)S(1)}, bf16[2,2048,128]{2,1,0:T(8,128)(2,1)S(1)}, ...), branch_computations={%region_8.9_spmd, %region_9.10_spmd, %region_10.11_spmd, %region_1... | conditional | flops 262145 | bytes 3145914 | solution.py:267
  24.7 1.3 %collective-permute-start.63 = (bf16[256,256]{1,0:T(8,128)(2,1)S(1)}, bf16[256,256]{1,0:T(8,128)(2,1)S(1)}, u32[]{:S(2)}, u32[]{:S(2)}) collective-permute-start(bf16[256,256]{1,0:T(8,128)(2,1)S(1)} %add_select_fusion.15), channel_id=1, source_target_pairs={{6,4},{14,0},{7,5},{15,1},{22,20},{30,16},{23,21},{31,17}} | collective-permute-start | bytes 393224 | tf_op jit(solution)/shard_map/cond/branch_7_fun/ppermute | solution.py:261
  27.3 1.9 %prepare.39 = bf16[1792,256]{1,0:T(8,128)(2,1)S(1)} custom-call(s32[4]{0:T(128)S(1)} %get-tuple-element.497.pivots_ref, bf16[4,2,256,256]{3,2,1,0:T(8,128)(2,1)S(1)} %get-tuple-element.498.inverse_ref, bf16[2,2048,128]{2,1,0:T(8,128)(2,1)S(1)} %get-tuple-element.499.refs_0_, bf16[2,2048,1024]{2,1,0:T(8,128)(2,1)} %get-tuple-element.500.refs_1_), custom_call_target="tpu_custom_call" | custom-call | tf_op jit(solution)/shard_map/cond/branch_7_fun/prepare/pallas_call | solution.py:90
  29.1 7.7 %collective-permute-done.63 = bf16[256,256]{1,0:T(8,128)(2,1)S(1)} collective-permute-done((bf16[256,256]{1,0:T(8,128)(2,1)S(1)}, bf16[256,256]{1,0:T(8,128)(2,1)S(1)}, u32[]{:S(2)}, u32[]{:S(2)}) %collective-permute-start.63) | collective-permute-done | bytes 131104 | tf_op jit(solution)/shard_map/cond/branch_7_fun/ppermute | solution.py:261
  37.5 12.9 %conditional.6 = (bf16[256,256]{1,0:T(8,128)(2,1)S(1)}, bf16[2304,256]{1,0:T(8,128)(2,1)S(1)}) conditional(s32[]{:T(128)} %bitcast.2, (s32[]{:T(128)}, bf16[256,256]{1,0:T(8,128)(2,1)S(1)}, s32[4]{0:T(128)S(1)}, bf16[4,2,256,256]{3,2,1,0:T(8,128)(2,1)S(1)}, bf16[2,2048,128]{2,1,0:T(8,128)(2,1)S(1)}, ...), branch_computations={%region_16.17_spmd, %region_17.18_spmd, %region_18.19_spmd, %regio... | conditional | flops 262145 | bytes 3145914 | solution.py:267
  41.0 2.0 %prepare.42 = bf16[2304,256]{1,0:T(8,128)(2,1)S(1)} custom-call(s32[4]{0:T(128)S(1)} %get-tuple-element.515.pivots_ref, bf16[4,2,256,256]{3,2,1,0:T(8,128)(2,1)S(1)} %get-tuple-element.516.inverse_ref, bf16[2,2048,128]{2,1,0:T(8,128)(2,1)S(1)} %get-tuple-element.517.refs_0_, bf16[2,2048,1024]{2,1,0:T(8,128)(2,1)} %get-tuple-element.518.refs_1_), custom_call_target="tpu_custom_call" | custom-call | tf_op jit(solution)/shard_map/cond/branch_2_fun/prepare/pallas_call | solution.py:90
  42.9 7.3 %collective-permute-done.74 = bf16[256,256]{1,0:T(8,128)(2,1)S(1)} collective-permute-done((bf16[256,256]{1,0:T(8,128)(2,1)S(1)}, bf16[256,256]{1,0:T(8,128)(2,1)S(1)}, u32[]{:S(2)}, u32[]{:S(2)}) %collective-permute-start.74) | collective-permute-done | bytes 131104 | tf_op jit(solution)/shard_map/cond/branch_2_fun/ppermute | solution.py:262
  51.2 16.2 %conditional.7 = (bf16[256,256]{1,0:T(8,128)(2,1)S(1)}, f32[256,2048]{1,0:T(8,128)S(1)}, bf16[2,2048,256]{2,1,0:T(8,128)(2,1)S(1)}) conditional(s32[]{:T(128)} %bitcast.1, (s32[]{:T(128)}, bf16[256,256]{1,0:T(8,128)(2,1)S(1)}, bf16[2,2048,128]{2,1,0:T(8,128)(2,1)S(1)}, bf16[2,2048,1024]{2,1,0:T(8,128)(2,1)}, ...), branch_computations={%region_24.25_spmd, %region_25.26_spmd, %region_26.27_spmd, %regio... | conditional | flops 262145 | bytes 3145922 | solution.py:267
  51.2 4.5 %collective-permute-start.97 = (bf16[256,256]{1,0:T(8,128)(2,1)S(1)}, bf16[256,256]{1,0:T(8,128)(2,1)S(1)}, u32[]{:S(2)}, u32[]{:S(2)}) collective-permute-start(bf16[256,256]{1,0:T(8,128)(2,1)S(1)} %get-tuple-element.550), channel_id=1, source_target_pairs={{0,8},{1,9},{16,24},{17,25}} | collective-permute-start | bytes 393224 | tf_op jit(solution)/shard_map/cond/branch_0_fun/ppermute | solution.py:257
  55.7 1.3 %collective-permute-start.96 = (bf16[256,256]{1,0:T(8,128)(2,1)S(1)}, bf16[256,256]{1,0:T(8,128)(2,1)S(1)}, u32[]{:S(2)}, u32[]{:S(2)}) collective-permute-start(bf16[256,256]{1,0:T(8,128)(2,1)S(1)} %get-tuple-element.550), channel_id=1, source_target_pairs={{0,2},{1,3},{16,18},{17,19}} | collective-permute-start | bytes 393224 | tf_op jit(solution)/shard_map/cond/branch_0_fun/ppermute | solution.py:257
  57.0 2.3 %collective-permute-done.97 = bf16[256,256]{1,0:T(8,128)(2,1)S(1)} collective-permute-done((bf16[256,256]{1,0:T(8,128)(2,1)S(1)}, bf16[256,256]{1,0:T(8,128)(2,1)S(1)}, u32[]{:S(2)}, u32[]{:S(2)}) %collective-permute-start.97) | collective-permute-done | bytes 131104 | tf_op jit(solution)/shard_map/cond/branch_0_fun/ppermute | solution.py:257
  59.5 1.3 %collective-permute-start.99 = (bf16[256,256]{1,0:T(8,128)(2,1)S(1)}, bf16[256,256]{1,0:T(8,128)(2,1)S(1)}, u32[]{:S(2)}, u32[]{:S(2)}) collective-permute-start(bf16[256,256]{1,0:T(8,128)(2,1)S(1)} %add_select_fusion.24), channel_id=1, source_target_pairs={{8,10},{0,14},{9,11},{1,15},{24,26},{16,30},{25,27},{17,31}} | collective-permute-start | bytes 393224 | tf_op jit(solution)/shard_map/cond/branch_0_fun/ppermute | solution.py:261
  60.8 1.3 %collective-permute-start.98 = (bf16[256,256]{1,0:T(8,128)(2,1)S(1)}, bf16[256,256]{1,0:T(8,128)(2,1)S(1)}, u32[]{:S(2)}, u32[]{:S(2)}) collective-permute-start(bf16[256,256]{1,0:T(8,128)(2,1)S(1)} %add_select_fusion.24), channel_id=1, source_target_pairs={{0,4},{2,6},{8,12},{10,14},{1,5},{3,7},{9,13},{11,15},{16,20},{18,... | collective-permute-start | bytes 393224 | tf_op jit(solution)/shard_map/cond/branch_0_fun/ppermute | solution.py:262
  62.1 5.2 %early_update.8 = (f32[256,2048]{1,0:T(8,128)S(1)}, bf16[2,2048,256]{2,1,0:T(8,128)(2,1)S(1)}) custom-call(bf16[2,2048,128]{2,1,0:T(8,128)(2,1)S(1)} %get-tuple-element.551.sides_ref, bf16[2,2048,1024]{2,1,0:T(8,128)(2,1)} %get-tuple-element.552.panel_ref, bf16[256,256]{1,0:T(8,128)(2,1)S(1)} %get-tuple-element.553.refs_0_, ...), custom_call_target="tpu_custom_call" | custom-call | tf_op jit(solution)/shard_map/cond/branch_0_fun/early_update/pallas_call | solution.py:158
  67.4 1.6 %last_update.1 = (bf16[2,16,2048]{2,1,0:T(8,128)(2,1)S(1)}, bf16[2,16,2048]{2,1,0:T(8,128)(2,1)S(1)}, bf16[2,16,2048]{2,1,0:T(8,128)(2,1)S(1)}, bf16[2,16,2048]{...) custom-call(s32[4]{0:T(128)S(1)} %copy-done.2, ...), custom_call_target="tpu_custom_call" | custom-call | tf_op jit(solution)/shard_map/last_update/pallas_call | solution.py:210
  69.0 1.9 %collective-permute-start.128 = (bf16[2,16,2048]{2,1,0:T(8,128)(2,1)S(1)}, bf16[2,16,2048]{2,1,0:T(8,128)(2,1)S(1)}, u32[]{:S(2)}, u32[]{:S(2)}) collective-permute-start(bf16[2,16,2048]{2,1,0:T(8,128)(2,1)S(1)} %get-tuple-element.658), channel_id=1, source_target_pairs={{0,2},{2,0},{4,6},{6,4},{8,10},{10,8},{12,14},{14,12},{1,3},{3,1},... | collective-permute-start | bytes 393224 | tf_op jit(solution)/shard_map/ppermute | solution.py:323
  72.6 3.5 %collective-permute-start.131 = (bf16[2,16,2048]{2,1,0:T(8,128)(2,1)S(1)}, bf16[2,16,2048]{2,1,0:T(8,128)(2,1)S(1)}, u32[]{:S(2)}, u32[]{:S(2)}) collective-permute-start(bf16[2,16,2048]{2,1,0:T(8,128)(2,1)S(1)} %get-tuple-element.661), channel_id=1, source_target_pairs={{0,8},{2,10},{4,12},{6,14},{8,0},{10,2},{12,4},{14,6},{1,9},{3,11}... | collective-permute-start | bytes 393224 | tf_op jit(solution)/shard_map/ppermute | solution.py:323
  76.7 4.2 %collective-permute-start.133 = (bf16[2,16,2048]{2,1,0:T(8,128)(2,1)S(1)}, bf16[2,16,2048]{2,1,0:T(8,128)(2,1)S(1)}, u32[]{:S(2)}, u32[]{:S(2)}) collective-permute-start(bf16[2,16,2048]{2,1,0:T(8,128)(2,1)S(1)} %get-tuple-element.663), channel_id=1, source_target_pairs={{0,12},{2,14},{4,8},{6,10},{8,4},{10,6},{12,0},{14,2},{1,13},{3,15... | collective-permute-start | bytes 393224 | tf_op jit(solution)/shard_map/ppermute | solution.py:323
  81.4 1.5 %collective-permute-done.130.refs_3_ = bf16[2,16,2048]{2,1,0:T(8,128)(2,1)S(1)} collective-permute-done((bf16[2,16,2048]{2,1,0:T(8,128)(2,1)S(1)}, bf16[2,16,2048]{2,1,0:T(8,128)(2,1)S(1)}, u32[]{:S(2)}, u32[]{:S(2)}) %collective-permute-start.130) | collective-permute-done | bytes 131104 | tf_op jit(solution)/shard_map/ppermute | solution.py:323
  82.9 6.6 %collective-permute-done.132.refs_5_ = bf16[2,16,2048]{2,1,0:T(8,128)(2,1)S(1)} collective-permute-done((bf16[2,16,2048]{2,1,0:T(8,128)(2,1)S(1)}, bf16[2,16,2048]{2,1,0:T(8,128)(2,1)S(1)}, u32[]{:S(2)}, u32[]{:S(2)}) %collective-permute-start.132) | collective-permute-done | bytes 131104 | tf_op jit(solution)/shard_map/ppermute | solution.py:323
  (50 shorter events, 16.0 us)
Async XLA Ops:
  0.0 4.9 %copy-start.1 = (bf16[4,2,256,256]{3,2,1,0:T(8,128)(2,1)S(1)}, bf16[4,2,256,256]{3,2,1,0:T(8,128)(2,1)}, u32[]{:S(2)}) copy-start(bf16[4,2,256,256]{3,2,1,0:T(8,128)(2,1)} %inverse_ref.1) | copy-start | bytes 3145732
  5.0 1.4 %collective-permute-start.29 = (bf16[256,256]{1,0:T(8,128)(2,1)S(1)}, bf16[256,256]{1,0:T(8,128)(2,1)S(1)}, u32[]{:S(2)}, u32[]{:S(2)}) collective-permute-start(bf16[256,256]{1,0:T(8,128)(2,1)S(1)} %get-tuple-element.448), channel_id=1, source_target_pairs={{14,6},{15,7},{30,22},{31,23}} | collective-permute-start | bytes 393224 | tf_op jit(solution)/shard_map/cond/branch_7_fun/ppermute | solution.py:257
  5.6 0.7 collective-permute-start.28
  6.4 16.3 %collective-permute-start.31 = (bf16[256,256]{1,0:T(8,128)(2,1)S(1)}, bf16[256,256]{1,0:T(8,128)(2,1)S(1)}, u32[]{:S(2)}, u32[]{:S(2)}) collective-permute-start(bf16[256,256]{1,0:T(8,128)(2,1)S(1)} %add_select_fusion.7), channel_id=1, source_target_pairs={{6,4},{14,0},{7,5},{15,1},{22,20},{30,16},{23,21},{31,17}} | collective-permute-start | bytes 393224 | tf_op jit(solution)/shard_map/cond/branch_7_fun/ppermute | solution.py:261
  7.7 15.0 %collective-permute-start.30 = (bf16[256,256]{1,0:T(8,128)(2,1)S(1)}, bf16[256,256]{1,0:T(8,128)(2,1)S(1)}, u32[]{:S(2)}, u32[]{:S(2)}) collective-permute-start(bf16[256,256]{1,0:T(8,128)(2,1)S(1)} %add_select_fusion.7), channel_id=1, source_target_pairs={{4,0},{6,2},{12,8},{14,10},{5,1},{7,3},{13,9},{15,11},{20,16},{22,... | collective-permute-start | bytes 393224 | tf_op jit(solution)/shard_map/cond/branch_7_fun/ppermute | solution.py:262
  23.3 1.4 %collective-permute-start.61 = (bf16[256,256]{1,0:T(8,128)(2,1)S(1)}, bf16[256,256]{1,0:T(8,128)(2,1)S(1)}, u32[]{:S(2)}, u32[]{:S(2)}) collective-permute-start(bf16[256,256]{1,0:T(8,128)(2,1)S(1)} %get-tuple-element.496), channel_id=1, source_target_pairs={{14,6},{15,7},{30,22},{31,23}} | collective-permute-start | bytes 393224 | tf_op jit(solution)/shard_map/cond/branch_7_fun/ppermute | solution.py:257
  23.9 0.7 collective-permute-start.60
  24.7 12.2 %collective-permute-start.63 = (bf16[256,256]{1,0:T(8,128)(2,1)S(1)}, bf16[256,256]{1,0:T(8,128)(2,1)S(1)}, u32[]{:S(2)}, u32[]{:S(2)}) collective-permute-start(bf16[256,256]{1,0:T(8,128)(2,1)S(1)} %add_select_fusion.15), channel_id=1, source_target_pairs={{6,4},{14,0},{7,5},{15,1},{22,20},{30,16},{23,21},{31,17}} | collective-permute-start | bytes 393224 | tf_op jit(solution)/shard_map/cond/branch_7_fun/ppermute | solution.py:261
  26.0 10.9 %collective-permute-start.62 = (bf16[256,256]{1,0:T(8,128)(2,1)S(1)}, bf16[256,256]{1,0:T(8,128)(2,1)S(1)}, u32[]{:S(2)}, u32[]{:S(2)}) collective-permute-start(bf16[256,256]{1,0:T(8,128)(2,1)S(1)} %add_select_fusion.15), channel_id=1, source_target_pairs={{4,0},{6,2},{12,8},{14,10},{5,1},{7,3},{13,9},{15,11},{20,16},{22,... | collective-permute-start | bytes 393224 | tf_op jit(solution)/shard_map/cond/branch_7_fun/ppermute | solution.py:262
  37.6 1.4 %collective-permute-start.73 = (bf16[256,256]{1,0:T(8,128)(2,1)S(1)}, bf16[256,256]{1,0:T(8,128)(2,1)S(1)}, u32[]{:S(2)}, u32[]{:S(2)}) collective-permute-start(bf16[256,256]{1,0:T(8,128)(2,1)S(1)} %get-tuple-element.514), channel_id=1, source_target_pairs={{4,12},{5,13},{20,28},{21,29}} | collective-permute-start | bytes 393224 | tf_op jit(solution)/shard_map/cond/branch_2_fun/ppermute | solution.py:257
  38.2 0.7 collective-permute-start.72
  39.0 3.9 %collective-permute-start.75 = (bf16[256,256]{1,0:T(8,128)(2,1)S(1)}, bf16[256,256]{1,0:T(8,128)(2,1)S(1)}, u32[]{:S(2)}, u32[]{:S(2)}) collective-permute-start(bf16[256,256]{1,0:T(8,128)(2,1)S(1)} %add_select_fusion.18), channel_id=1, source_target_pairs={{12,14},{4,10},{13,15},{5,11},{28,30},{20,26},{29,31},{21,27}} | collective-permute-start | bytes 393224 | tf_op jit(solution)/shard_map/cond/branch_2_fun/ppermute | solution.py:261
  39.7 10.6 %collective-permute-start.74 = (bf16[256,256]{1,0:T(8,128)(2,1)S(1)}, bf16[256,256]{1,0:T(8,128)(2,1)S(1)}, u32[]{:S(2)}, u32[]{:S(2)}) collective-permute-start(bf16[256,256]{1,0:T(8,128)(2,1)S(1)} %add_select_fusion.18), channel_id=1, source_target_pairs={{4,0},{6,2},{12,8},{14,10},{5,1},{7,3},{13,9},{15,11},{20,16},{22,... | collective-permute-start | bytes 393224 | tf_op jit(solution)/shard_map/cond/branch_2_fun/ppermute | solution.py:262
  51.2 8.1 %collective-permute-start.97 = (bf16[256,256]{1,0:T(8,128)(2,1)S(1)}, bf16[256,256]{1,0:T(8,128)(2,1)S(1)}, u32[]{:S(2)}, u32[]{:S(2)}) collective-permute-start(bf16[256,256]{1,0:T(8,128)(2,1)S(1)} %get-tuple-element.550), channel_id=1, source_target_pairs={{0,8},{1,9},{16,24},{17,25}} | collective-permute-start | bytes 393224 | tf_op jit(solution)/shard_map/cond/branch_0_fun/ppermute | solution.py:257
  55.7 3.8 %collective-permute-start.96 = (bf16[256,256]{1,0:T(8,128)(2,1)S(1)}, bf16[256,256]{1,0:T(8,128)(2,1)S(1)}, u32[]{:S(2)}, u32[]{:S(2)}) collective-permute-start(bf16[256,256]{1,0:T(8,128)(2,1)S(1)} %get-tuple-element.550), channel_id=1, source_target_pairs={{0,2},{1,3},{16,18},{17,19}} | collective-permute-start | bytes 393224 | tf_op jit(solution)/shard_map/cond/branch_0_fun/ppermute | solution.py:257
  59.5 7.8 %collective-permute-start.99 = (bf16[256,256]{1,0:T(8,128)(2,1)S(1)}, bf16[256,256]{1,0:T(8,128)(2,1)S(1)}, u32[]{:S(2)}, u32[]{:S(2)}) collective-permute-start(bf16[256,256]{1,0:T(8,128)(2,1)S(1)} %add_select_fusion.24), channel_id=1, source_target_pairs={{8,10},{0,14},{9,11},{1,15},{24,26},{16,30},{25,27},{17,31}} | collective-permute-start | bytes 393224 | tf_op jit(solution)/shard_map/cond/branch_0_fun/ppermute | solution.py:261
  60.8 6.5 %collective-permute-start.98 = (bf16[256,256]{1,0:T(8,128)(2,1)S(1)}, bf16[256,256]{1,0:T(8,128)(2,1)S(1)}, u32[]{:S(2)}, u32[]{:S(2)}) collective-permute-start(bf16[256,256]{1,0:T(8,128)(2,1)S(1)} %add_select_fusion.24), channel_id=1, source_target_pairs={{0,4},{2,6},{8,12},{10,14},{1,5},{3,7},{9,13},{11,15},{16,20},{18,... | collective-permute-start | bytes 393224 | tf_op jit(solution)/shard_map/cond/branch_0_fun/ppermute | solution.py:262
  69.0 7.7 %collective-permute-start.128 = (bf16[2,16,2048]{2,1,0:T(8,128)(2,1)S(1)}, bf16[2,16,2048]{2,1,0:T(8,128)(2,1)S(1)}, u32[]{:S(2)}, u32[]{:S(2)}) collective-permute-start(bf16[2,16,2048]{2,1,0:T(8,128)(2,1)S(1)} %get-tuple-element.658), channel_id=1, source_target_pairs={{0,2},{2,0},{4,6},{6,4},{8,10},{10,8},{12,14},{14,12},{1,3},{3,1},... | collective-permute-start | bytes 393224 | tf_op jit(solution)/shard_map/ppermute | solution.py:323
  70.9 10.0 %collective-permute-start.129 = (bf16[2,16,2048]{2,1,0:T(8,128)(2,1)S(1)}, bf16[2,16,2048]{2,1,0:T(8,128)(2,1)S(1)}, u32[]{:S(2)}, u32[]{:S(2)}) collective-permute-start(bf16[2,16,2048]{2,1,0:T(8,128)(2,1)S(1)} %get-tuple-element.659), channel_id=1, source_target_pairs={{0,4},{2,6},{4,0},{6,2},{8,12},{10,14},{12,8},{14,10},{1,5},{3,7},... | collective-permute-start | bytes 393224 | tf_op jit(solution)/shard_map/ppermute | solution.py:323
  71.9 11.1 %collective-permute-start.130 = (bf16[2,16,2048]{2,1,0:T(8,128)(2,1)S(1)}, bf16[2,16,2048]{2,1,0:T(8,128)(2,1)S(1)}, u32[]{:S(2)}, u32[]{:S(2)}) collective-permute-start(bf16[2,16,2048]{2,1,0:T(8,128)(2,1)S(1)} %get-tuple-element.660), channel_id=1, source_target_pairs={{0,6},{2,4},{4,2},{6,0},{8,14},{10,12},{12,10},{14,8},{1,7},{3,5},... | collective-permute-start | bytes 393224 | tf_op jit(solution)/shard_map/ppermute | solution.py:323
  72.6 10.4 %collective-permute-start.131 = (bf16[2,16,2048]{2,1,0:T(8,128)(2,1)S(1)}, bf16[2,16,2048]{2,1,0:T(8,128)(2,1)S(1)}, u32[]{:S(2)}, u32[]{:S(2)}) collective-permute-start(bf16[2,16,2048]{2,1,0:T(8,128)(2,1)S(1)} %get-tuple-element.661), channel_id=1, source_target_pairs={{0,8},{2,10},{4,12},{6,14},{8,0},{10,2},{12,4},{14,6},{1,9},{3,11}... | collective-permute-start | bytes 393224 | tf_op jit(solution)/shard_map/ppermute | solution.py:323
  76.0 13.6 %collective-permute-start.132 = (bf16[2,16,2048]{2,1,0:T(8,128)(2,1)S(1)}, bf16[2,16,2048]{2,1,0:T(8,128)(2,1)S(1)}, u32[]{:S(2)}, u32[]{:S(2)}) collective-permute-start(bf16[2,16,2048]{2,1,0:T(8,128)(2,1)S(1)} %get-tuple-element.662), channel_id=1, source_target_pairs={{0,10},{2,8},{4,14},{6,12},{8,2},{10,0},{12,6},{14,4},{1,11},{3,9}... | collective-permute-start | bytes 393224 | tf_op jit(solution)/shard_map/ppermute | solution.py:323
  76.7 12.8 %collective-permute-start.133 = (bf16[2,16,2048]{2,1,0:T(8,128)(2,1)S(1)}, bf16[2,16,2048]{2,1,0:T(8,128)(2,1)S(1)}, u32[]{:S(2)}, u32[]{:S(2)}) collective-permute-start(bf16[2,16,2048]{2,1,0:T(8,128)(2,1)S(1)} %get-tuple-element.663), channel_id=1, source_target_pairs={{0,12},{2,14},{4,8},{6,10},{8,4},{10,6},{12,0},{14,2},{1,13},{3,15... | collective-permute-start | bytes 393224 | tf_op jit(solution)/shard_map/ppermute | solution.py:323
  80.9 8.7 %collective-permute-start.134 = (bf16[2,16,2048]{2,1,0:T(8,128)(2,1)S(1)}, bf16[2,16,2048]{2,1,0:T(8,128)(2,1)S(1)}, u32[]{:S(2)}, u32[]{:S(2)}) collective-permute-start(bf16[2,16,2048]{2,1,0:T(8,128)(2,1)S(1)} %get-tuple-element.664), channel_id=1, source_target_pairs={{0,14},{2,12},{4,10},{6,8},{8,6},{10,4},{12,2},{14,0},{1,15},{3,13... | collective-permute-start | bytes 393224 | tf_op jit(solution)/shard_map/ppermute | solution.py:323
  (2 other events, 9.8 us)

commit v3 on v2

--- a/solution.py
+++ b/solution.py
@@ -254,13 +254,13 @@
 
     def branch(source):
         def run(value):
-            early = [lax.ppermute(value, "rows", [(source, source ^ step)]) for step in (1, 4)]
-            have = jnp.where(me == source, value, early[0] + early[1])
+            early = [lax.ppermute(value, "rows", [(source, source ^ step)]) for step in (7, 1, 4)]
+            have = jnp.where(me == source, value, early[1] + early[2])
             results = beside()
             corner = [source ^ step for step in (0, 1, 4, 5)]
-            fourth = lax.ppermute(have, "rows", [(source ^ 4, source ^ 5), (source, source ^ 7)])
+            fourth = lax.ppermute(have, "rows", [(source ^ 4, source ^ 5)])
             third = lax.ppermute(have, "rows", sorted((device, device ^ 2) for device in corner))
-            return have + third + fourth, results
+            return have + early[0] + third + fourth, results
 
         return run
 

time: 92.4 us -> 91.1 us (0.986)
  waiting for transfers between devices: 37.7 us -> 31.1 us
  starting transfers between devices: 31.9 us -> 35.4 us
    ppermute x4, waiting for transfers between devices: 19.7 us -> 0.01 us  [run(): fourth = lax.ppermute(have, 'rows', [(source ^ 4, source ^ 5)])]
    ppermute x8 -> x12, waiting for transfers between devices: 2.51 us -> 9.36 us  [run(): lax.ppermute(value, 'rows', [(source, source ^ step)])]
    ppermute x4, waiting for transfers between devices: 7.33 us -> 13.7 us  [run(): lax.ppermute(have, 'rows', sorted(((device, device ^ 2) for device in cor...]
    ppermute x8 -> x12, starting transfers between devices: 9.78 us -> 15.9 us  [run(): lax.ppermute(value, 'rows', [(source, source ^ step)])]
    ppermute x4, starting transfers between devices: 4.55 us -> 2.68 us  [run(): fourth = lax.ppermute(have, 'rows', [(source ^ 4, source ^ 5)])]
    add x4, other arithmetic: 0.09 us -> 1.02 us  [run(): return (have + early[0] + third + fourth, results)]
  transfers between devices with their start and end apart: 23 -> 27, of which waited for: 7 -> 8; matrix products, arithmetic and copies ran while one was open for 0% -> 0% of each run, Pallas kernels for 12% -> 12%
where the time goes in v3:
time: 91.1 us; the launch traced here: 89.4 us
  starting transfers between devices  35.4 us (39%)
  waiting for transfers between devices  31.1 us (34%)
  Pallas kernels  17.6 us (19%)
  between operations  2.8 us (3%)
  other arithmetic  1.1 us (1%)
    ppermute x12, starting transfers between devices, run(): lax.ppermute(value, 'rows', [(source, source ^ step)])  15.9 us
    ppermute x4, waiting for transfers between devices, run(): lax.ppermute(have, 'rows', sorted(((device, device ^ 2) for device in cor...  13.7 us
    ppermute x7, starting transfers between devices, body(): lax.ppermute(blocks[step], 'rows', [(i, i ^ step) for i in range(ranks)])  11.7 us
    ppermute x12, waiting for transfers between devices, run(): lax.ppermute(value, 'rows', [(source, source ^ step)])  9.36 us
    ppermute x7, waiting for transfers between devices, body(): lax.ppermute(blocks[step], 'rows', [(i, i ^ step) for i in range(ranks)])  8.09 us
    pallas_call x3, Pallas kernels, prepare(): pl.pallas_call(functools.partial(prepare_kernel, numbers), out_shape=[jax...  5.55 us
    pallas_call x1, Pallas kernels, early_update(): pl.pallas_call(early_kernel, out_shape=[jax.ShapeDtypeStruct((height, loc...  5.19 us
    ppermute x4, starting transfers between devices, run(): lax.ppermute(have, 'rows', sorted(((device, device ^ 2) for device in cor...  5.17 us
  transfers between devices with their start and end apart: 27, of which 8 were waited for; matrix products, arithmetic and copies ran while one was open for 0% of the time, Pallas kernels for 12%

profile of v3, /device:TPU:0, one launch (start us, length us, event | category | flops | bytes accessed | tf_op | source)
XLA Modules:
  0.0 89.4 jit_solution(6095302974905579163)
XLA Ops:
  0.0 2.4 %solve_first.1 = (bf16[256,256]{1,0:T(8,128)(2,1)S(1)}, s32[1]{0:T(128)}, s32[1]{0:T(128)}, s32[1]{0:T(128)}, s32[1]{0:T(128)}) custom-call(s32[4]{0:T(128)} %pivots_ref.3, bf16[2,2048,128]{2,1,0:T(8,128)(2,1)} %sides_ref.1, bf16[4,2,256,256]{3,2,1,0:T(8,128)(2,1)} %inverse_ref.1), custom_call_target="tpu_custom_call" | custom-call | tf_op jit(solution)/shard_map/solve_first/pallas_call | solution.py:47
  4.9 14.9 %conditional.4 = (bf16[256,256]{1,0:T(8,128)(2,1)S(1)}, bf16[1280,256]{1,0:T(8,128)(2,1)S(1)}) conditional(s32[]{:T(128)} %bitcast.4, (s32[]{:T(128)}, bf16[256,256]{1,0:T(8,128)(2,1)S(1)}, s32[4]{0:T(128)S(1)}, bf16[4,2,256,256]{3,2,1,0:T(8,128)(2,1)S(1)}, bf16[2,2048,128]{2,1,0:T(8,128)(2,1)S(1)}, ...), branch_computations={%region_0.1_spmd, %region_1.2_spmd, %region_2.3_spmd, %region_3.4_... | conditional | flops 327681 | bytes 3801314 | solution.py:267
  5.0 6.0 %collective-permute-start.1 = (bf16[256,256]{1,0:T(8,128)(2,1)S(1)}, bf16[256,256]{1,0:T(8,128)(2,1)S(1)}, u32[]{:S(2)}, u32[]{:S(2)}) collective-permute-start(bf16[256,256]{1,0:T(8,128)(2,1)S(1)} %get-tuple-element.406), channel_id=1, source_target_pairs={{0,8},{1,9},{16,24},{17,25}} | collective-permute-start | bytes 393224 | tf_op jit(solution)/shard_map/cond/branch_0_fun/ppermute | solution.py:257
  10.9 1.3 %collective-permute-start = (bf16[256,256]{1,0:T(8,128)(2,1)S(1)}, bf16[256,256]{1,0:T(8,128)(2,1)S(1)}, u32[]{:S(2)}, u32[]{:S(2)}) collective-permute-start(bf16[256,256]{1,0:T(8,128)(2,1)S(1)} %get-tuple-element.406), channel_id=1, source_target_pairs={{0,2},{1,3},{16,18},{17,19}} | collective-permute-start | bytes 393224 | tf_op jit(solution)/shard_map/cond/branch_0_fun/ppermute | solution.py:257
  12.2 2.0 %collective-permute-start.2 = (bf16[256,256]{1,0:T(8,128)(2,1)S(1)}, bf16[256,256]{1,0:T(8,128)(2,1)S(1)}, u32[]{:S(2)}, u32[]{:S(2)}) collective-permute-start(bf16[256,256]{1,0:T(8,128)(2,1)S(1)} %get-tuple-element.406), channel_id=1, source_target_pairs={{0,14},{1,15},{16,30},{17,31}} | collective-permute-start | bytes 393224 | tf_op jit(solution)/shard_map/cond/branch_0_fun/ppermute | solution.py:257
  15.7 1.3 %collective-permute-start.3 = (bf16[256,256]{1,0:T(8,128)(2,1)S(1)}, bf16[256,256]{1,0:T(8,128)(2,1)S(1)}, u32[]{:S(2)}, u32[]{:S(2)}) collective-permute-start(bf16[256,256]{1,0:T(8,128)(2,1)S(1)} %add_select_fusion), channel_id=1, source_target_pairs={{0,4},{2,6},{8,12},{10,14},{1,5},{3,7},{9,13},{11,15},{16,20},{18,... | collective-permute-start | bytes 393224 | tf_op jit(solution)/shard_map/cond/branch_0_fun/ppermute | solution.py:262
  17.0 1.7 %prepare.24 = bf16[1280,256]{1,0:T(8,128)(2,1)S(1)} custom-call(s32[4]{0:T(128)S(1)} %get-tuple-element.407.pivots_ref, bf16[4,2,256,256]{3,2,1,0:T(8,128)(2,1)S(1)} %get-tuple-element.408.inverse_ref, bf16[2,2048,128]{2,1,0:T(8,128)(2,1)S(1)} %get-tuple-element.409.refs_0_, bf16[2,2048,1024]{2,1,0:T(8,128)(2,1)} %get-tuple-element.410.refs_1_), custom_call_target="tpu_custom_call" | custom-call | tf_op jit(solution)/shard_map/cond/branch_0_fun/prepare/pallas_call | solution.py:90
  20.4 16.8 %conditional.5 = (bf16[256,256]{1,0:T(8,128)(2,1)S(1)}, bf16[1792,256]{1,0:T(8,128)(2,1)S(1)}) conditional(s32[]{:T(128)} %bitcast.3, (s32[]{:T(128)}, bf16[256,256]{1,0:T(8,128)(2,1)S(1)}, s32[4]{0:T(128)S(1)}, bf16[4,2,256,256]{3,2,1,0:T(8,128)(2,1)S(1)}, bf16[2,2048,128]{2,1,0:T(8,128)(2,1)S(1)}, ...), branch_computations={%region_8.9_spmd, %region_9.10_spmd, %region_10.11_spmd, %region_1... | conditional | flops 327681 | bytes 4325630 | solution.py:267
  25.1 1.9 %prepare.39 = bf16[1792,256]{1,0:T(8,128)(2,1)S(1)} custom-call(s32[4]{0:T(128)S(1)} %get-tuple-element.497.pivots_ref, bf16[4,2,256,256]{3,2,1,0:T(8,128)(2,1)S(1)} %get-tuple-element.498.inverse_ref, bf16[2,2048,128]{2,1,0:T(8,128)(2,1)S(1)} %get-tuple-element.499.refs_0_, bf16[2,2048,1024]{2,1,0:T(8,128)(2,1)} %get-tuple-element.500.refs_1_), custom_call_target="tpu_custom_call" | custom-call | tf_op jit(solution)/shard_map/cond/branch_7_fun/prepare/pallas_call | solution.py:90
  27.0 8.6 %collective-permute-done.77 = bf16[256,256]{1,0:T(8,128)(2,1)S(1)} collective-permute-done((bf16[256,256]{1,0:T(8,128)(2,1)S(1)}, bf16[256,256]{1,0:T(8,128)(2,1)S(1)}, u32[]{:S(2)}, u32[]{:S(2)}) %collective-permute-start.77) | collective-permute-done | bytes 131104 | tf_op jit(solution)/shard_map/cond/branch_7_fun/ppermute | solution.py:257
  37.9 14.7 %conditional.6 = (bf16[256,256]{1,0:T(8,128)(2,1)S(1)}, bf16[2304,256]{1,0:T(8,128)(2,1)S(1)}) conditional(s32[]{:T(128)} %bitcast.2, (s32[]{:T(128)}, bf16[256,256]{1,0:T(8,128)(2,1)S(1)}, s32[4]{0:T(128)S(1)}, bf16[4,2,256,256]{3,2,1,0:T(8,128)(2,1)S(1)}, bf16[2,2048,128]{2,1,0:T(8,128)(2,1)S(1)}, ...), branch_computations={%region_16.17_spmd, %region_17.18_spmd, %region_18.19_spmd, %regio... | conditional | flops 327681 | bytes 3801314 | solution.py:267
  42.0 2.0 %prepare.43 = bf16[2304,256]{1,0:T(8,128)(2,1)S(1)} custom-call(s32[4]{0:T(128)S(1)} %get-tuple-element.521.pivots_ref, bf16[4,2,256,256]{3,2,1,0:T(8,128)(2,1)S(1)} %get-tuple-element.522.inverse_ref, bf16[2,2048,128]{2,1,0:T(8,128)(2,1)S(1)} %get-tuple-element.523.refs_0_, bf16[2,2048,1024]{2,1,0:T(8,128)(2,1)} %get-tuple-element.524.refs_1_), custom_call_target="tpu_custom_call" | custom-call | tf_op jit(solution)/shard_map/cond/branch_3_fun/prepare/pallas_call | solution.py:90
  43.9 8.4 %collective-permute-done.98 = bf16[256,256]{1,0:T(8,128)(2,1)S(1)} collective-permute-done((bf16[256,256]{1,0:T(8,128)(2,1)S(1)}, bf16[256,256]{1,0:T(8,128)(2,1)S(1)}, u32[]{:S(2)}, u32[]{:S(2)}) %collective-permute-start.98) | collective-permute-done | bytes 131104 | tf_op jit(solution)/shard_map/cond/branch_3_fun/ppermute | solution.py:262
  53.3 13.5 %conditional.7 = (bf16[256,256]{1,0:T(8,128)(2,1)S(1)}, f32[256,2048]{1,0:T(8,128)S(1)}, bf16[2,2048,256]{2,1,0:T(8,128)(2,1)S(1)}) conditional(s32[]{:T(128)} %bitcast.1, (s32[]{:T(128)}, bf16[256,256]{1,0:T(8,128)(2,1)S(1)}, bf16[2,2048,128]{2,1,0:T(8,128)(2,1)S(1)}, bf16[2,2048,1024]{2,1,0:T(8,128)(2,1)}, ...), branch_computations={%region_24.25_spmd, %region_25.26_spmd, %region_26.27_spmd, %regio... | conditional | flops 327681 | bytes 3801322 | solution.py:267
  57.4 5.2 %early_update.11 = (f32[256,2048]{1,0:T(8,128)S(1)}, bf16[2,2048,256]{2,1,0:T(8,128)(2,1)S(1)}) custom-call(bf16[2,2048,128]{2,1,0:T(8,128)(2,1)S(1)} %get-tuple-element.578.sides_ref, bf16[2,2048,1024]{2,1,0:T(8,128)(2,1)} %get-tuple-element.579.panel_ref, bf16[256,256]{1,0:T(8,128)(2,1)S(1)} %get-tuple-element.580.refs_0_, ...), custom_call_target="tpu_custom_call" | custom-call | tf_op jit(solution)/shard_map/cond/branch_3_fun/early_update/pallas_call | solution.py:158
  62.6 4.2 %collective-permute-done.138 = bf16[256,256]{1,0:T(8,128)(2,1)S(1)} collective-permute-done((bf16[256,256]{1,0:T(8,128)(2,1)S(1)}, bf16[256,256]{1,0:T(8,128)(2,1)S(1)}, u32[]{:S(2)}, u32[]{:S(2)}) %collective-permute-start.138) | collective-permute-done | bytes 131104 | tf_op jit(solution)/shard_map/cond/branch_3_fun/ppermute | solution.py:262
  66.8 1.6 %last_update.1 = (bf16[2,16,2048]{2,1,0:T(8,128)(2,1)S(1)}, bf16[2,16,2048]{2,1,0:T(8,128)(2,1)S(1)}, bf16[2,16,2048]{2,1,0:T(8,128)(2,1)S(1)}, bf16[2,16,2048]{...) custom-call(s32[4]{0:T(128)S(1)} %copy-done.2, ...), custom_call_target="tpu_custom_call" | custom-call | tf_op jit(solution)/shard_map/last_update/pallas_call | solution.py:210
  68.5 1.4 %collective-permute-start.161 = (bf16[2,16,2048]{2,1,0:T(8,128)(2,1)S(1)}, bf16[2,16,2048]{2,1,0:T(8,128)(2,1)S(1)}, u32[]{:S(2)}, u32[]{:S(2)}) collective-permute-start(bf16[2,16,2048]{2,1,0:T(8,128)(2,1)S(1)} %get-tuple-element.659), channel_id=1, source_target_pairs={{0,4},{2,6},{4,0},{6,2},{8,12},{10,14},{12,8},{14,10},{1,5},{3,7},... | collective-permute-start | bytes 393224 | tf_op jit(solution)/shard_map/ppermute | solution.py:323
  70.0 2.0 %collective-permute-start.162 = (bf16[2,16,2048]{2,1,0:T(8,128)(2,1)S(1)}, bf16[2,16,2048]{2,1,0:T(8,128)(2,1)S(1)}, u32[]{:S(2)}, u32[]{:S(2)}) collective-permute-start(bf16[2,16,2048]{2,1,0:T(8,128)(2,1)S(1)} %get-tuple-element.660), channel_id=1, source_target_pairs={{0,6},{2,4},{4,2},{6,0},{8,14},{10,12},{12,10},{14,8},{1,7},{3,5},... | collective-permute-start | bytes 393224 | tf_op jit(solution)/shard_map/ppermute | solution.py:323
  72.3 2.1 %collective-permute-start.164 = (bf16[2,16,2048]{2,1,0:T(8,128)(2,1)S(1)}, bf16[2,16,2048]{2,1,0:T(8,128)(2,1)S(1)}, u32[]{:S(2)}, u32[]{:S(2)}) collective-permute-start(bf16[2,16,2048]{2,1,0:T(8,128)(2,1)S(1)} %get-tuple-element.662), channel_id=1, source_target_pairs={{0,10},{2,8},{4,14},{6,12},{8,2},{10,0},{12,6},{14,4},{1,11},{3,9}... | collective-permute-start | bytes 393224 | tf_op jit(solution)/shard_map/ppermute | solution.py:323
  74.4 3.0 %collective-permute-start.165 = (bf16[2,16,2048]{2,1,0:T(8,128)(2,1)S(1)}, bf16[2,16,2048]{2,1,0:T(8,128)(2,1)S(1)}, u32[]{:S(2)}, u32[]{:S(2)}) collective-permute-start(bf16[2,16,2048]{2,1,0:T(8,128)(2,1)S(1)} %get-tuple-element.663), channel_id=1, source_target_pairs={{0,12},{2,14},{4,8},{6,10},{8,4},{10,6},{12,0},{14,2},{1,13},{3,15... | collective-permute-start | bytes 393224 | tf_op jit(solution)/shard_map/ppermute | solution.py:323
  78.7 2.7 %collective-permute-start.166 = (bf16[2,16,2048]{2,1,0:T(8,128)(2,1)S(1)}, bf16[2,16,2048]{2,1,0:T(8,128)(2,1)S(1)}, u32[]{:S(2)}, u32[]{:S(2)}) collective-permute-start(bf16[2,16,2048]{2,1,0:T(8,128)(2,1)S(1)} %get-tuple-element.664), channel_id=1, source_target_pairs={{0,14},{2,12},{4,10},{6,8},{8,6},{10,4},{12,2},{14,0},{1,15},{3,13... | collective-permute-start | bytes 393224 | tf_op jit(solution)/shard_map/ppermute | solution.py:323
  81.4 2.4 %collective-permute-done.163.refs_4_ = bf16[2,16,2048]{2,1,0:T(8,128)(2,1)S(1)} collective-permute-done((bf16[2,16,2048]{2,1,0:T(8,128)(2,1)S(1)}, bf16[2,16,2048]{2,1,0:T(8,128)(2,1)S(1)}, u32[]{:S(2)}, u32[]{:S(2)}) %collective-permute-start.163) | collective-permute-done | bytes 131104 | tf_op jit(solution)/shard_map/ppermute | solution.py:323
  83.8 4.4 %collective-permute-done.164.refs_5_ = bf16[2,16,2048]{2,1,0:T(8,128)(2,1)S(1)} collective-permute-done((bf16[2,16,2048]{2,1,0:T(8,128)(2,1)S(1)}, bf16[2,16,2048]{2,1,0:T(8,128)(2,1)S(1)}, u32[]{:S(2)}, u32[]{:S(2)}) %collective-permute-start.164) | collective-permute-done | bytes 131104 | tf_op jit(solution)/shard_map/ppermute | solution.py:323
  (60 shorter events, 21.2 us)
Async XLA Ops:
  5.0 9.3 %collective-permute-start.1 = (bf16[256,256]{1,0:T(8,128)(2,1)S(1)}, bf16[256,256]{1,0:T(8,128)(2,1)S(1)}, u32[]{:S(2)}, u32[]{:S(2)}) collective-permute-start(bf16[256,256]{1,0:T(8,128)(2,1)S(1)} %get-tuple-element.406), channel_id=1, source_target_pairs={{0,8},{1,9},{16,24},{17,25}} | collective-permute-start | bytes 393224 | tf_op jit(solution)/shard_map/cond/branch_0_fun/ppermute | solution.py:257
  10.9 4.0 %collective-permute-start = (bf16[256,256]{1,0:T(8,128)(2,1)S(1)}, bf16[256,256]{1,0:T(8,128)(2,1)S(1)}, u32[]{:S(2)}, u32[]{:S(2)}) collective-permute-start(bf16[256,256]{1,0:T(8,128)(2,1)S(1)} %get-tuple-element.406), channel_id=1, source_target_pairs={{0,2},{1,3},{16,18},{17,19}} | collective-permute-start | bytes 393224 | tf_op jit(solution)/shard_map/cond/branch_0_fun/ppermute | solution.py:257
  12.2 6.5 %collective-permute-start.2 = (bf16[256,256]{1,0:T(8,128)(2,1)S(1)}, bf16[256,256]{1,0:T(8,128)(2,1)S(1)}, u32[]{:S(2)}, u32[]{:S(2)}) collective-permute-start(bf16[256,256]{1,0:T(8,128)(2,1)S(1)} %get-tuple-element.406), channel_id=1, source_target_pairs={{0,14},{1,15},{16,30},{17,31}} | collective-permute-start | bytes 393224 | tf_op jit(solution)/shard_map/cond/branch_0_fun/ppermute | solution.py:257
  15.0 3.7 %collective-permute-start.4 = (bf16[256,256]{1,0:T(8,128)(2,1)S(1)}, bf16[256,256]{1,0:T(8,128)(2,1)S(1)}, u32[]{:S(2)}, u32[]{:S(2)}) collective-permute-start(bf16[256,256]{1,0:T(8,128)(2,1)S(1)} %add_select_fusion), channel_id=1, source_target_pairs={{8,10},{9,11},{24,26},{25,27}} | collective-permute-start | bytes 393224 | tf_op jit(solution)/shard_map/cond/branch_0_fun/ppermute | solution.py:261
  15.7 4.1 %collective-permute-start.3 = (bf16[256,256]{1,0:T(8,128)(2,1)S(1)}, bf16[256,256]{1,0:T(8,128)(2,1)S(1)}, u32[]{:S(2)}, u32[]{:S(2)}) collective-permute-start(bf16[256,256]{1,0:T(8,128)(2,1)S(1)} %add_select_fusion), channel_id=1, source_target_pairs={{0,4},{2,6},{8,12},{10,14},{1,5},{3,7},{9,13},{11,15},{16,20},{18,... | collective-permute-start | bytes 393224 | tf_op jit(solution)/shard_map/cond/branch_0_fun/ppermute | solution.py:262
  20.4 2.7 %collective-permute-start.76 = (bf16[256,256]{1,0:T(8,128)(2,1)S(1)}, bf16[256,256]{1,0:T(8,128)(2,1)S(1)}, u32[]{:S(2)}, u32[]{:S(2)}) collective-permute-start(bf16[256,256]{1,0:T(8,128)(2,1)S(1)} %get-tuple-element.496), channel_id=1, source_target_pairs={{14,6},{15,7},{30,22},{31,23}} | collective-permute-start | bytes 393224 | tf_op jit(solution)/shard_map/cond/branch_7_fun/ppermute | solution.py:257
  21.8 13.8 %collective-permute-start.77 = (bf16[256,256]{1,0:T(8,128)(2,1)S(1)}, bf16[256,256]{1,0:T(8,128)(2,1)S(1)}, u32[]{:S(2)}, u32[]{:S(2)}) collective-permute-start(bf16[256,256]{1,0:T(8,128)(2,1)S(1)} %get-tuple-element.496), channel_id=1, source_target_pairs={{14,0},{15,1},{30,16},{31,17}} | collective-permute-start | bytes 393224 | tf_op jit(solution)/shard_map/cond/branch_7_fun/ppermute | solution.py:257
  23.2 12.5 %collective-permute-start.79 = (bf16[256,256]{1,0:T(8,128)(2,1)S(1)}, bf16[256,256]{1,0:T(8,128)(2,1)S(1)}, u32[]{:S(2)}, u32[]{:S(2)}) collective-permute-start(bf16[256,256]{1,0:T(8,128)(2,1)S(1)} %add_select_fusion.15), channel_id=1, source_target_pairs={{6,4},{7,5},{22,20},{23,21}} | collective-permute-start | bytes 393224 | tf_op jit(solution)/shard_map/cond/branch_7_fun/ppermute | solution.py:261
  23.8 12.5 %collective-permute-start.78 = (bf16[256,256]{1,0:T(8,128)(2,1)S(1)}, bf16[256,256]{1,0:T(8,128)(2,1)S(1)}, u32[]{:S(2)}, u32[]{:S(2)}) collective-permute-start(bf16[256,256]{1,0:T(8,128)(2,1)S(1)} %add_select_fusion.15), channel_id=1, source_target_pairs={{4,0},{6,2},{12,8},{14,10},{5,1},{7,3},{13,9},{15,11},{20,16},{22,... | collective-permute-start | bytes 393224 | tf_op jit(solution)/shard_map/cond/branch_7_fun/ppermute | solution.py:262
  37.9 2.0 %collective-permute-start.96 = (bf16[256,256]{1,0:T(8,128)(2,1)S(1)}, bf16[256,256]{1,0:T(8,128)(2,1)S(1)}, u32[]{:S(2)}, u32[]{:S(2)}) collective-permute-start(bf16[256,256]{1,0:T(8,128)(2,1)S(1)} %get-tuple-element.520), channel_id=1, source_target_pairs={{6,14},{7,15},{22,30},{23,31}} | collective-permute-start | bytes 393224 | tf_op jit(solution)/shard_map/cond/branch_3_fun/ppermute | solution.py:257
  39.2 4.7 %collective-permute-start.97 = (bf16[256,256]{1,0:T(8,128)(2,1)S(1)}, bf16[256,256]{1,0:T(8,128)(2,1)S(1)}, u32[]{:S(2)}, u32[]{:S(2)}) collective-permute-start(bf16[256,256]{1,0:T(8,128)(2,1)S(1)} %get-tuple-element.520), channel_id=1, source_target_pairs={{6,8},{7,9},{22,24},{23,25}} | collective-permute-start | bytes 393224 | tf_op jit(solution)/shard_map/cond/branch_3_fun/ppermute | solution.py:257
  40.0 4.0 %collective-permute-start.99 = (bf16[256,256]{1,0:T(8,128)(2,1)S(1)}, bf16[256,256]{1,0:T(8,128)(2,1)S(1)}, u32[]{:S(2)}, u32[]{:S(2)}) collective-permute-start(bf16[256,256]{1,0:T(8,128)(2,1)S(1)} %add_select_fusion.19), channel_id=1, source_target_pairs={{14,12},{15,13},{30,28},{31,29}} | collective-permute-start | bytes 393224 | tf_op jit(solution)/shard_map/cond/branch_3_fun/ppermute | solution.py:261
  40.7 11.7 %collective-permute-start.98 = (bf16[256,256]{1,0:T(8,128)(2,1)S(1)}, bf16[256,256]{1,0:T(8,128)(2,1)S(1)}, u32[]{:S(2)}, u32[]{:S(2)}) collective-permute-start(bf16[256,256]{1,0:T(8,128)(2,1)S(1)} %add_select_fusion.19), channel_id=1, source_target_pairs={{4,0},{6,2},{12,8},{14,10},{5,1},{7,3},{13,9},{15,11},{20,16},{22,... | collective-permute-start | bytes 393224 | tf_op jit(solution)/shard_map/cond/branch_3_fun/ppermute | solution.py:262
  53.3 2.0 %collective-permute-start.136 = (bf16[256,256]{1,0:T(8,128)(2,1)S(1)}, bf16[256,256]{1,0:T(8,128)(2,1)S(1)}, u32[]{:S(2)}, u32[]{:S(2)}) collective-permute-start(bf16[256,256]{1,0:T(8,128)(2,1)S(1)} %get-tuple-element.577), channel_id=1, source_target_pairs={{6,14},{7,15},{22,30},{23,31}} | collective-permute-start | bytes 393224 | tf_op jit(solution)/shard_map/cond/branch_3_fun/ppermute | solution.py:257
  54.7 7.9 %collective-permute-start.137 = (bf16[256,256]{1,0:T(8,128)(2,1)S(1)}, bf16[256,256]{1,0:T(8,128)(2,1)S(1)}, u32[]{:S(2)}, u32[]{:S(2)}) collective-permute-start(bf16[256,256]{1,0:T(8,128)(2,1)S(1)} %get-tuple-element.577), channel_id=1, source_target_pairs={{6,8},{7,9},{22,24},{23,25}} | collective-permute-start | bytes 393224 | tf_op jit(solution)/shard_map/cond/branch_3_fun/ppermute | solution.py:257
  55.4 7.2 %collective-permute-start.139 = (bf16[256,256]{1,0:T(8,128)(2,1)S(1)}, bf16[256,256]{1,0:T(8,128)(2,1)S(1)}, u32[]{:S(2)}, u32[]{:S(2)}) collective-permute-start(bf16[256,256]{1,0:T(8,128)(2,1)S(1)} %add_select_fusion.27), channel_id=1, source_target_pairs={{14,12},{15,13},{30,28},{31,29}} | collective-permute-start | bytes 393224 | tf_op jit(solution)/shard_map/cond/branch_3_fun/ppermute | solution.py:261
  56.1 10.7 %collective-permute-start.138 = (bf16[256,256]{1,0:T(8,128)(2,1)S(1)}, bf16[256,256]{1,0:T(8,128)(2,1)S(1)}, u32[]{:S(2)}, u32[]{:S(2)}) collective-permute-start(bf16[256,256]{1,0:T(8,128)(2,1)S(1)} %add_select_fusion.27), channel_id=1, source_target_pairs={{4,0},{6,2},{12,8},{14,10},{5,1},{7,3},{13,9},{15,11},{20,16},{22,... | collective-permute-start | bytes 393224 | tf_op jit(solution)/shard_map/cond/branch_3_fun/ppermute | solution.py:262
  68.4 6.0 %collective-permute-start.160 = (bf16[2,16,2048]{2,1,0:T(8,128)(2,1)S(1)}, bf16[2,16,2048]{2,1,0:T(8,128)(2,1)S(1)}, u32[]{:S(2)}, u32[]{:S(2)}) collective-permute-start(bf16[2,16,2048]{2,1,0:T(8,128)(2,1)S(1)} %get-tuple-element.658), channel_id=1, source_target_pairs={{0,2},{2,0},{4,6},{6,4},{8,10},{10,8},{12,14},{14,12},{1,3},{3,1},... | collective-permute-start | bytes 393224 | tf_op jit(solution)/shard_map/ppermute | solution.py:323
  68.5 10.1 %collective-permute-start.161 = (bf16[2,16,2048]{2,1,0:T(8,128)(2,1)S(1)}, bf16[2,16,2048]{2,1,0:T(8,128)(2,1)S(1)}, u32[]{:S(2)}, u32[]{:S(2)}) collective-permute-start(bf16[2,16,2048]{2,1,0:T(8,128)(2,1)S(1)} %get-tuple-element.659), channel_id=1, source_target_pairs={{0,4},{2,6},{4,0},{6,2},{8,12},{10,14},{12,8},{14,10},{1,5},{3,7},... | collective-permute-start | bytes 393224 | tf_op jit(solution)/shard_map/ppermute | solution.py:323
  70.0 11.4 %collective-permute-start.162 = (bf16[2,16,2048]{2,1,0:T(8,128)(2,1)S(1)}, bf16[2,16,2048]{2,1,0:T(8,128)(2,1)S(1)}, u32[]{:S(2)}, u32[]{:S(2)}) collective-permute-start(bf16[2,16,2048]{2,1,0:T(8,128)(2,1)S(1)} %get-tuple-element.660), channel_id=1, source_target_pairs={{0,6},{2,4},{4,2},{6,0},{8,14},{10,12},{12,10},{14,8},{1,7},{3,5},... | collective-permute-start | bytes 393224 | tf_op jit(solution)/shard_map/ppermute | solution.py:323
  72.0 11.8 %collective-permute-start.163 = (bf16[2,16,2048]{2,1,0:T(8,128)(2,1)S(1)}, bf16[2,16,2048]{2,1,0:T(8,128)(2,1)S(1)}, u32[]{:S(2)}, u32[]{:S(2)}) collective-permute-start(bf16[2,16,2048]{2,1,0:T(8,128)(2,1)S(1)} %get-tuple-element.661), channel_id=1, source_target_pairs={{0,8},{2,10},{4,12},{6,14},{8,0},{10,2},{12,4},{14,6},{1,9},{3,11}... | collective-permute-start | bytes 393224 | tf_op jit(solution)/shard_map/ppermute | solution.py:323
  72.3 15.9 %collective-permute-start.164 = (bf16[2,16,2048]{2,1,0:T(8,128)(2,1)S(1)}, bf16[2,16,2048]{2,1,0:T(8,128)(2,1)S(1)}, u32[]{:S(2)}, u32[]{:S(2)}) collective-permute-start(bf16[2,16,2048]{2,1,0:T(8,128)(2,1)S(1)} %get-tuple-element.662), channel_id=1, source_target_pairs={{0,10},{2,8},{4,14},{6,12},{8,2},{10,0},{12,6},{14,4},{1,11},{3,9}... | collective-permute-start | bytes 393224 | tf_op jit(solution)/shard_map/ppermute | solution.py:323
  74.4 13.8 %collective-permute-start.165 = (bf16[2,16,2048]{2,1,0:T(8,128)(2,1)S(1)}, bf16[2,16,2048]{2,1,0:T(8,128)(2,1)S(1)}, u32[]{:S(2)}, u32[]{:S(2)}) collective-permute-start(bf16[2,16,2048]{2,1,0:T(8,128)(2,1)S(1)} %get-tuple-element.663), channel_id=1, source_target_pairs={{0,12},{2,14},{4,8},{6,10},{8,4},{10,6},{12,0},{14,2},{1,13},{3,15... | collective-permute-start | bytes 393224 | tf_op jit(solution)/shard_map/ppermute | solution.py:323
  78.7 9.6 %collective-permute-start.166 = (bf16[2,16,2048]{2,1,0:T(8,128)(2,1)S(1)}, bf16[2,16,2048]{2,1,0:T(8,128)(2,1)S(1)}, u32[]{:S(2)}, u32[]{:S(2)}) collective-permute-start(bf16[2,16,2048]{2,1,0:T(8,128)(2,1)S(1)} %get-tuple-element.664), channel_id=1, source_target_pairs={{0,14},{2,12},{4,10},{6,8},{8,6},{10,4},{12,2},{14,0},{1,15},{3,13... | collective-permute-start | bytes 393224 | tf_op jit(solution)/shard_map/ppermute | solution.py:323
  (7 other events, 20.2 us)

commit v4 on v3

--- a/solution.py
+++ b/solution.py
@@ -9,7 +9,7 @@
 
 CONTRACT_LAST = (((1,), (1,)), ((), ()))
 
-BESIDE_PANELS = pltpu.CompilerParams(vmem_limit_bytes=40 * 1024 * 1024)
+BESIDE_PANELS = pltpu.CompilerParams(vmem_limit_bytes=52 * 1024 * 1024)
 TILES = 4
 RANKS = 8
 SMALL = pltpu.CompilerParams(vmem_limit_bytes=16 * 1024 * 1024)

time: 91.1 us -> 91.1 us (level); the launches traced: 89.4 us -> 91.2 us
  starting transfers between devices: 35.4 us -> 37.5 us
    ppermute x4, waiting for transfers between devices: 13.7 us -> 1.67 us  [run(): lax.ppermute(have, 'rows', sorted(((device, device ^ 2) for device in cor...]
    ppermute x12, waiting for transfers between devices: 9.36 us -> 19.6 us  [run(): lax.ppermute(value, 'rows', [(source, source ^ step)])]
    ppermute x7, waiting for transfers between devices: 8.09 us -> 10.2 us  [body(): lax.ppermute(blocks[step], 'rows', [(i, i ^ step) for i in range(ranks)])]
    ppermute x12, starting transfers between devices: 15.9 us -> 17.8 us  [run(): lax.ppermute(value, 'rows', [(source, source ^ step)])]
  transfers between devices with their start and end apart: 27 -> 27, of which waited for: 8 -> 9; matrix products, arithmetic and copies ran while one was open for 0% -> 0% of each run, Pallas kernels for 12% -> 12%
where the time goes in v4:
time: 91.1 us; the launch traced here: 91.2 us
  starting transfers between devices  37.5 us (41%)
  waiting for transfers between devices  31.5 us (35%)
  Pallas kernels  17.6 us (19%)
  between operations  2.81 us (3%)
  other arithmetic  1.1 us (1%)
    ppermute x12, waiting for transfers between devices, run(): lax.ppermute(value, 'rows', [(source, source ^ step)])  19.6 us
    ppermute x12, starting transfers between devices, run(): lax.ppermute(value, 'rows', [(source, source ^ step)])  17.8 us
    ppermute x7, starting transfers between devices, body(): lax.ppermute(blocks[step], 'rows', [(i, i ^ step) for i in range(ranks)])  11.2 us
    ppermute x7, waiting for transfers between devices, body(): lax.ppermute(blocks[step], 'rows', [(i, i ^ step) for i in range(ranks)])  10.2 us
    pallas_call x3, Pallas kernels, prepare(): pl.pallas_call(functools.partial(prepare_kernel, numbers), out_shape=[jax...  5.55 us
    pallas_call x1, Pallas kernels, early_update(): pl.pallas_call(early_kernel, out_shape=[jax.ShapeDtypeStruct((height, loc...  5.19 us
    ppermute x4, starting transfers between devices, run(): lax.ppermute(have, 'rows', sorted(((device, device ^ 2) for device in cor...  5.18 us
    ppermute x4, starting transfers between devices, run(): fourth = lax.ppermute(have, 'rows', [(source ^ 4, source ^ 5)])  3.3 us
  transfers between devices with their start and end apart: 27, of which 9 were waited for; matrix products, arithmetic and copies ran while one was open for 0% of the time, Pallas kernels for 12%

profile of v4, /device:TPU:0, one launch (start us, length us, event | category | flops | bytes accessed | tf_op | source)
XLA Modules:
  0.0 91.2 jit_solution(17955906149170378637)
XLA Ops:
  0.0 2.4 %solve_first.1 = (bf16[256,256]{1,0:T(8,128)(2,1)S(1)}, s32[1]{0:T(128)}, s32[1]{0:T(128)}, s32[1]{0:T(128)}, s32[1]{0:T(128)}) custom-call(s32[4]{0:T(128)} %pivots_ref.3, bf16[2,2048,128]{2,1,0:T(8,128)(2,1)} %sides_ref.1, bf16[4,2,256,256]{3,2,1,0:T(8,128)(2,1)} %inverse_ref.1), custom_call_target="tpu_custom_call" | custom-call | tf_op jit(solution)/shard_map/solve_first/pallas_call | solution.py:47
  4.9 14.9 %conditional.4 = (bf16[256,256]{1,0:T(8,128)(2,1)S(1)}, bf16[1280,256]{1,0:T(8,128)(2,1)S(1)}) conditional(s32[]{:T(128)} %bitcast.4, (s32[]{:T(128)}, bf16[256,256]{1,0:T(8,128)(2,1)S(1)}, s32[4]{0:T(128)S(1)}, bf16[4,2,256,256]{3,2,1,0:T(8,128)(2,1)S(1)}, bf16[2,2048,128]{2,1,0:T(8,128)(2,1)S(1)}, ...), branch_computations={%region_0.1_spmd, %region_1.2_spmd, %region_2.3_spmd, %region_3.4_... | conditional | flops 327681 | bytes 3801314 | solution.py:267
  5.0 6.0 %collective-permute-start.1 = (bf16[256,256]{1,0:T(8,128)(2,1)S(1)}, bf16[256,256]{1,0:T(8,128)(2,1)S(1)}, u32[]{:S(2)}, u32[]{:S(2)}) collective-permute-start(bf16[256,256]{1,0:T(8,128)(2,1)S(1)} %get-tuple-element.406), channel_id=1, source_target_pairs={{0,8},{1,9},{16,24},{17,25}} | collective-permute-start | bytes 393224 | tf_op jit(solution)/shard_map/cond/branch_0_fun/ppermute | solution.py:257
  10.9 1.3 %collective-permute-start = (bf16[256,256]{1,0:T(8,128)(2,1)S(1)}, bf16[256,256]{1,0:T(8,128)(2,1)S(1)}, u32[]{:S(2)}, u32[]{:S(2)}) collective-permute-start(bf16[256,256]{1,0:T(8,128)(2,1)S(1)} %get-tuple-element.406), channel_id=1, source_target_pairs={{0,2},{1,3},{16,18},{17,19}} | collective-permute-start | bytes 393224 | tf_op jit(solution)/shard_map/cond/branch_0_fun/ppermute | solution.py:257
  12.2 2.0 %collective-permute-start.2 = (bf16[256,256]{1,0:T(8,128)(2,1)S(1)}, bf16[256,256]{1,0:T(8,128)(2,1)S(1)}, u32[]{:S(2)}, u32[]{:S(2)}) collective-permute-start(bf16[256,256]{1,0:T(8,128)(2,1)S(1)} %get-tuple-element.406), channel_id=1, source_target_pairs={{0,14},{1,15},{16,30},{17,31}} | collective-permute-start | bytes 393224 | tf_op jit(solution)/shard_map/cond/branch_0_fun/ppermute | solution.py:257
  17.0 1.7 %prepare.24 = bf16[1280,256]{1,0:T(8,128)(2,1)S(1)} custom-call(s32[4]{0:T(128)S(1)} %get-tuple-element.407.pivots_ref, bf16[4,2,256,256]{3,2,1,0:T(8,128)(2,1)S(1)} %get-tuple-element.408.inverse_ref, bf16[2,2048,128]{2,1,0:T(8,128)(2,1)S(1)} %get-tuple-element.409.refs_0_, bf16[2,2048,1024]{2,1,0:T(8,128)(2,1)} %get-tuple-element.410.refs_1_), custom_call_target="tpu_custom_call" | custom-call | tf_op jit(solution)/shard_map/cond/branch_0_fun/prepare/pallas_call | solution.py:90
  20.4 15.2 %conditional.5 = (bf16[256,256]{1,0:T(8,128)(2,1)S(1)}, bf16[1792,256]{1,0:T(8,128)(2,1)S(1)}) conditional(s32[]{:T(128)} %bitcast.3, (s32[]{:T(128)}, bf16[256,256]{1,0:T(8,128)(2,1)S(1)}, s32[4]{0:T(128)S(1)}, bf16[4,2,256,256]{3,2,1,0:T(8,128)(2,1)S(1)}, bf16[2,2048,128]{2,1,0:T(8,128)(2,1)S(1)}, ...), branch_computations={%region_8.9_spmd, %region_9.10_spmd, %region_10.11_spmd, %region_1... | conditional | flops 327681 | bytes 4325630 | solution.py:267
  22.4 1.3 %collective-permute-start.47 = (bf16[256,256]{1,0:T(8,128)(2,1)S(1)}, bf16[256,256]{1,0:T(8,128)(2,1)}, u32[]{:S(2)}, u32[]{:S(2)}) collective-permute-start(bf16[256,256]{1,0:T(8,128)(2,1)S(1)} %get-tuple-element.460), channel_id=1, source_target_pairs={{2,12},{3,13},{18,28},{19,29}} | collective-permute-start | bytes 393224 | tf_op jit(solution)/shard_map/cond/branch_1_fun/ppermute | solution.py:257
  23.7 6.4 %collective-permute-done.45 = bf16[256,256]{1,0:T(8,128)(2,1)S(1)} collective-permute-done((bf16[256,256]{1,0:T(8,128)(2,1)S(1)}, bf16[256,256]{1,0:T(8,128)(2,1)S(1)}, u32[]{:S(2)}, u32[]{:S(2)}) %collective-permute-start.45) | collective-permute-done | bytes 131104 | tf_op jit(solution)/shard_map/cond/branch_1_fun/ppermute | solution.py:257
  32.1 1.8 %prepare.33 = bf16[1792,256]{1,0:T(8,128)(2,1)S(1)} custom-call(s32[4]{0:T(128)S(1)} %get-tuple-element.461.pivots_ref, bf16[4,2,256,256]{3,2,1,0:T(8,128)(2,1)S(1)} %get-tuple-element.462.inverse_ref, bf16[2,2048,128]{2,1,0:T(8,128)(2,1)S(1)} %get-tuple-element.463.refs_0_, bf16[2,2048,1024]{2,1,0:T(8,128)(2,1)} %get-tuple-element.464.refs_1_), custom_call_target="tpu_custom_call" | custom-call | tf_op jit(solution)/shard_map/cond/branch_1_fun/prepare/pallas_call | solution.py:90
  36.2 13.6 %conditional.6 = (bf16[256,256]{1,0:T(8,128)(2,1)S(1)}, bf16[2304,256]{1,0:T(8,128)(2,1)S(1)}) conditional(s32[]{:T(128)} %bitcast.2, (s32[]{:T(128)}, bf16[256,256]{1,0:T(8,128)(2,1)S(1)}, s32[4]{0:T(128)S(1)}, bf16[4,2,256,256]{3,2,1,0:T(8,128)(2,1)S(1)}, bf16[2,2048,128]{2,1,0:T(8,128)(2,1)S(1)}, ...), branch_computations={%region_16.17_spmd, %region_17.18_spmd, %region_18.19_spmd, %regio... | conditional | flops 327681 | bytes 3801314 | solution.py:267
  41.1 2.0 %prepare.47 = bf16[2304,256]{1,0:T(8,128)(2,1)S(1)} custom-call(s32[4]{0:T(128)S(1)} %get-tuple-element.545.pivots_ref, bf16[4,2,256,256]{3,2,1,0:T(8,128)(2,1)S(1)} %get-tuple-element.546.inverse_ref, bf16[2,2048,128]{2,1,0:T(8,128)(2,1)S(1)} %get-tuple-element.547.refs_0_, bf16[2,2048,1024]{2,1,0:T(8,128)(2,1)} %get-tuple-element.548.refs_1_), custom_call_target="tpu_custom_call" | custom-call | tf_op jit(solution)/shard_map/cond/branch_7_fun/prepare/pallas_call | solution.py:90
  43.1 6.7 %collective-permute-done.117 = bf16[256,256]{1,0:T(8,128)(2,1)S(1)} collective-permute-done((bf16[256,256]{1,0:T(8,128)(2,1)S(1)}, bf16[256,256]{1,0:T(8,128)(2,1)S(1)}, u32[]{:S(2)}, u32[]{:S(2)}) %collective-permute-start.117) | collective-permute-done | bytes 131104 | tf_op jit(solution)/shard_map/cond/branch_7_fun/ppermute | solution.py:257
  50.5 16.4 %conditional.7 = (bf16[256,256]{1,0:T(8,128)(2,1)S(1)}, f32[256,2048]{1,0:T(8,128)S(1)}, bf16[2,2048,256]{2,1,0:T(8,128)(2,1)S(1)}) conditional(s32[]{:T(128)} %bitcast.1, (s32[]{:T(128)}, bf16[256,256]{1,0:T(8,128)(2,1)S(1)}, bf16[2,2048,128]{2,1,0:T(8,128)(2,1)S(1)}, bf16[2,2048,1024]{2,1,0:T(8,128)(2,1)}, ...), branch_computations={%region_24.25_spmd, %region_25.26_spmd, %region_26.27_spmd, %regio... | conditional | flops 327681 | bytes 3801322 | solution.py:267
  53.2 5.8 %collective-permute-done.141 = bf16[256,256]{1,0:T(8,128)(2,1)S(1)} collective-permute-done((bf16[256,256]{1,0:T(8,128)(2,1)S(1)}, bf16[256,256]{1,0:T(8,128)(2,1)S(1)}, u32[]{:S(2)}, u32[]{:S(2)}) %collective-permute-start.141) | collective-permute-done | bytes 131104 | tf_op jit(solution)/shard_map/cond/branch_4_fun/ppermute | solution.py:257
  61.7 5.2 %early_update.12 = (f32[256,2048]{1,0:T(8,128)S(1)}, bf16[2,2048,256]{2,1,0:T(8,128)(2,1)S(1)}) custom-call(bf16[2,2048,128]{2,1,0:T(8,128)(2,1)S(1)} %get-tuple-element.587.sides_ref, bf16[2,2048,1024]{2,1,0:T(8,128)(2,1)} %get-tuple-element.588.panel_ref, bf16[256,256]{1,0:T(8,128)(2,1)S(1)} %get-tuple-element.589.refs_0_, ...), custom_call_target="tpu_custom_call" | custom-call | tf_op jit(solution)/shard_map/cond/branch_4_fun/early_update/pallas_call | solution.py:158
  67.0 1.6 %last_update.1 = (bf16[2,16,2048]{2,1,0:T(8,128)(2,1)S(1)}, bf16[2,16,2048]{2,1,0:T(8,128)(2,1)S(1)}, bf16[2,16,2048]{2,1,0:T(8,128)(2,1)S(1)}, bf16[2,16,2048]{...) custom-call(s32[4]{0:T(128)S(1)} %copy-done.2, ...), custom_call_target="tpu_custom_call" | custom-call | tf_op jit(solution)/shard_map/last_update/pallas_call | solution.py:210
  68.7 3.4 %collective-permute-start.162 = (bf16[2,16,2048]{2,1,0:T(8,128)(2,1)S(1)}, bf16[2,16,2048]{2,1,0:T(8,128)(2,1)S(1)}, u32[]{:S(2)}, u32[]{:S(2)}) collective-permute-start(bf16[2,16,2048]{2,1,0:T(8,128)(2,1)S(1)} %get-tuple-element.660), channel_id=1, source_target_pairs={{0,6},{2,4},{4,2},{6,0},{8,14},{10,12},{12,10},{14,8},{1,7},{3,5},... | collective-permute-start | bytes 393224 | tf_op jit(solution)/shard_map/ppermute | solution.py:323
  72.1 2.4 %collective-permute-start.164 = (bf16[2,16,2048]{2,1,0:T(8,128)(2,1)S(1)}, bf16[2,16,2048]{2,1,0:T(8,128)(2,1)S(1)}, u32[]{:S(2)}, u32[]{:S(2)}) collective-permute-start(bf16[2,16,2048]{2,1,0:T(8,128)(2,1)S(1)} %get-tuple-element.662), channel_id=1, source_target_pairs={{0,10},{2,8},{4,14},{6,12},{8,2},{10,0},{12,6},{14,4},{1,11},{3,9}... | collective-permute-start | bytes 393224 | tf_op jit(solution)/shard_map/ppermute | solution.py:323
  74.6 1.3 %collective-permute-start.165 = (bf16[2,16,2048]{2,1,0:T(8,128)(2,1)S(1)}, bf16[2,16,2048]{2,1,0:T(8,128)(2,1)S(1)}, u32[]{:S(2)}, u32[]{:S(2)}) collective-permute-start(bf16[2,16,2048]{2,1,0:T(8,128)(2,1)S(1)} %get-tuple-element.663), channel_id=1, source_target_pairs={{0,12},{2,14},{4,8},{6,10},{8,4},{10,6},{12,0},{14,2},{1,13},{3,15... | collective-permute-start | bytes 393224 | tf_op jit(solution)/shard_map/ppermute | solution.py:323
  75.9 3.9 %collective-permute-start.166 = (bf16[2,16,2048]{2,1,0:T(8,128)(2,1)S(1)}, bf16[2,16,2048]{2,1,0:T(8,128)(2,1)S(1)}, u32[]{:S(2)}, u32[]{:S(2)}) collective-permute-start(bf16[2,16,2048]{2,1,0:T(8,128)(2,1)S(1)} %get-tuple-element.664), channel_id=1, source_target_pairs={{0,14},{2,12},{4,10},{6,8},{8,6},{10,4},{12,2},{14,0},{1,15},{3,13... | collective-permute-start | bytes 393224 | tf_op jit(solution)/shard_map/ppermute | solution.py:323
  79.8 1.6 %collective-permute-done.162.refs_3_ = bf16[2,16,2048]{2,1,0:T(8,128)(2,1)S(1)} collective-permute-done((bf16[2,16,2048]{2,1,0:T(8,128)(2,1)S(1)}, bf16[2,16,2048]{2,1,0:T(8,128)(2,1)S(1)}, u32[]{:S(2)}, u32[]{:S(2)}) %collective-permute-start.162) | collective-permute-done | bytes 131104 | tf_op jit(solution)/shard_map/ppermute | solution.py:323
  81.4 6.0 %collective-permute-done.163.refs_4_ = bf16[2,16,2048]{2,1,0:T(8,128)(2,1)S(1)} collective-permute-done((bf16[2,16,2048]{2,1,0:T(8,128)(2,1)S(1)}, bf16[2,16,2048]{2,1,0:T(8,128)(2,1)S(1)}, u32[]{:S(2)}, u32[]{:S(2)}) %collective-permute-start.163) | collective-permute-done | bytes 131104 | tf_op jit(solution)/shard_map/ppermute | solution.py:323
  87.3 2.7 %collective-permute-done.164.refs_5_ = bf16[2,16,2048]{2,1,0:T(8,128)(2,1)S(1)} collective-permute-done((bf16[2,16,2048]{2,1,0:T(8,128)(2,1)S(1)}, bf16[2,16,2048]{2,1,0:T(8,128)(2,1)S(1)}, u32[]{:S(2)}, u32[]{:S(2)}) %collective-permute-start.164) | collective-permute-done | bytes 131104 | tf_op jit(solution)/shard_map/ppermute | solution.py:323
  (58 shorter events, 22.3 us)
Async XLA Ops:
  5.0 9.3 %collective-permute-start.1 = (bf16[256,256]{1,0:T(8,128)(2,1)S(1)}, bf16[256,256]{1,0:T(8,128)(2,1)S(1)}, u32[]{:S(2)}, u32[]{:S(2)}) collective-permute-start(bf16[256,256]{1,0:T(8,128)(2,1)S(1)} %get-tuple-element.406), channel_id=1, source_target_pairs={{0,8},{1,9},{16,24},{17,25}} | collective-permute-start | bytes 393224 | tf_op jit(solution)/shard_map/cond/branch_0_fun/ppermute | solution.py:257
  10.9 4.0 %collective-permute-start = (bf16[256,256]{1,0:T(8,128)(2,1)S(1)}, bf16[256,256]{1,0:T(8,128)(2,1)S(1)}, u32[]{:S(2)}, u32[]{:S(2)}) collective-permute-start(bf16[256,256]{1,0:T(8,128)(2,1)S(1)} %get-tuple-element.406), channel_id=1, source_target_pairs={{0,2},{1,3},{16,18},{17,19}} | collective-permute-start | bytes 393224 | tf_op jit(solution)/shard_map/cond/branch_0_fun/ppermute | solution.py:257
  12.2 6.5 %collective-permute-start.2 = (bf16[256,256]{1,0:T(8,128)(2,1)S(1)}, bf16[256,256]{1,0:T(8,128)(2,1)S(1)}, u32[]{:S(2)}, u32[]{:S(2)}) collective-permute-start(bf16[256,256]{1,0:T(8,128)(2,1)S(1)} %get-tuple-element.406), channel_id=1, source_target_pairs={{0,14},{1,15},{16,30},{17,31}} | collective-permute-start | bytes 393224 | tf_op jit(solution)/shard_map/cond/branch_0_fun/ppermute | solution.py:257
  15.0 3.7 %collective-permute-start.4 = (bf16[256,256]{1,0:T(8,128)(2,1)S(1)}, bf16[256,256]{1,0:T(8,128)(2,1)S(1)}, u32[]{:S(2)}, u32[]{:S(2)}) collective-permute-start(bf16[256,256]{1,0:T(8,128)(2,1)S(1)} %add_select_fusion), channel_id=1, source_target_pairs={{8,10},{9,11},{24,26},{25,27}} | collective-permute-start | bytes 393224 | tf_op jit(solution)/shard_map/cond/branch_0_fun/ppermute | solution.py:261
  15.7 4.1 %collective-permute-start.3 = (bf16[256,256]{1,0:T(8,128)(2,1)S(1)}, bf16[256,256]{1,0:T(8,128)(2,1)S(1)}, u32[]{:S(2)}, u32[]{:S(2)}) collective-permute-start(bf16[256,256]{1,0:T(8,128)(2,1)S(1)} %add_select_fusion), channel_id=1, source_target_pairs={{0,4},{2,6},{8,12},{10,14},{1,5},{3,7},{9,13},{11,15},{16,20},{18,... | collective-permute-start | bytes 393224 | tf_op jit(solution)/shard_map/cond/branch_0_fun/ppermute | solution.py:262
  21.1 9.0 %collective-permute-start.45 = (bf16[256,256]{1,0:T(8,128)(2,1)S(1)}, bf16[256,256]{1,0:T(8,128)(2,1)S(1)}, u32[]{:S(2)}, u32[]{:S(2)}) collective-permute-start(bf16[256,256]{1,0:T(8,128)(2,1)S(1)} %get-tuple-element.460), channel_id=1, source_target_pairs={{2,0},{3,1},{18,16},{19,17}} | collective-permute-start | bytes 393224 | tf_op jit(solution)/shard_map/cond/branch_1_fun/ppermute | solution.py:257
  22.4 11.6 %collective-permute-start.47 = (bf16[256,256]{1,0:T(8,128)(2,1)S(1)}, bf16[256,256]{1,0:T(8,128)(2,1)}, u32[]{:S(2)}, u32[]{:S(2)}) collective-permute-start(bf16[256,256]{1,0:T(8,128)(2,1)S(1)} %get-tuple-element.460), channel_id=1, source_target_pairs={{2,12},{3,13},{18,28},{19,29}} | collective-permute-start | bytes 393224 | tf_op jit(solution)/shard_map/cond/branch_1_fun/ppermute | solution.py:257
  30.1 3.9 %collective-permute-start.49 = (bf16[256,256]{1,0:T(8,128)(2,1)S(1)}, bf16[256,256]{1,0:T(8,128)(2,1)S(1)}, u32[]{:S(2)}, u32[]{:S(2)}) collective-permute-start(bf16[256,256]{1,0:T(8,128)(2,1)S(1)} %add_select_fusion.9), channel_id=1, source_target_pairs={{10,8},{11,9},{26,24},{27,25}} | collective-permute-start | bytes 393224 | tf_op jit(solution)/shard_map/cond/branch_1_fun/ppermute | solution.py:261
  30.8 3.8 %collective-permute-start.48 = (bf16[256,256]{1,0:T(8,128)(2,1)S(1)}, bf16[256,256]{1,0:T(8,128)(2,1)S(1)}, u32[]{:S(2)}, u32[]{:S(2)}) collective-permute-start(bf16[256,256]{1,0:T(8,128)(2,1)S(1)} %add_select_fusion.9), channel_id=1, source_target_pairs={{0,4},{2,6},{8,12},{10,14},{1,5},{3,7},{9,13},{11,15},{16,20},{18,... | collective-permute-start | bytes 393224 | tf_op jit(solution)/shard_map/cond/branch_1_fun/ppermute | solution.py:262
  37.8 12.0 %collective-permute-start.117 = (bf16[256,256]{1,0:T(8,128)(2,1)S(1)}, bf16[256,256]{1,0:T(8,128)(2,1)S(1)}, u32[]{:S(2)}, u32[]{:S(2)}) collective-permute-start(bf16[256,256]{1,0:T(8,128)(2,1)S(1)} %get-tuple-element.544), channel_id=1, source_target_pairs={{14,0},{15,1},{30,16},{31,17}} | collective-permute-start | bytes 393224 | tf_op jit(solution)/shard_map/cond/branch_7_fun/ppermute | solution.py:257
  39.1 10.6 %collective-permute-start.119 = (bf16[256,256]{1,0:T(8,128)(2,1)S(1)}, bf16[256,256]{1,0:T(8,128)(2,1)S(1)}, u32[]{:S(2)}, u32[]{:S(2)}) collective-permute-start(bf16[256,256]{1,0:T(8,128)(2,1)S(1)} %add_select_fusion.23), channel_id=1, source_target_pairs={{6,4},{7,5},{22,20},{23,21}} | collective-permute-start | bytes 393224 | tf_op jit(solution)/shard_map/cond/branch_7_fun/ppermute | solution.py:261
  39.8 10.0 %collective-permute-start.118 = (bf16[256,256]{1,0:T(8,128)(2,1)S(1)}, bf16[256,256]{1,0:T(8,128)(2,1)S(1)}, u32[]{:S(2)}, u32[]{:S(2)}) collective-permute-start(bf16[256,256]{1,0:T(8,128)(2,1)S(1)} %add_select_fusion.23), channel_id=1, source_target_pairs={{4,0},{6,2},{12,8},{14,10},{5,1},{7,3},{13,9},{15,11},{20,16},{22,... | collective-permute-start | bytes 393224 | tf_op jit(solution)/shard_map/cond/branch_7_fun/ppermute | solution.py:262
  50.5 8.5 %collective-permute-start.141 = (bf16[256,256]{1,0:T(8,128)(2,1)S(1)}, bf16[256,256]{1,0:T(8,128)(2,1)S(1)}, u32[]{:S(2)}, u32[]{:S(2)}) collective-permute-start(bf16[256,256]{1,0:T(8,128)(2,1)S(1)} %get-tuple-element.586), channel_id=1, source_target_pairs={{8,0},{9,1},{24,16},{25,17}} | collective-permute-start | bytes 393224 | tf_op jit(solution)/shard_map/cond/branch_4_fun/ppermute | solution.py:257
  51.8 7.2 %collective-permute-start.140 = (bf16[256,256]{1,0:T(8,128)(2,1)S(1)}, bf16[256,256]{1,0:T(8,128)(2,1)S(1)}, u32[]{:S(2)}, u32[]{:S(2)}) collective-permute-start(bf16[256,256]{1,0:T(8,128)(2,1)S(1)} %get-tuple-element.586), channel_id=1, source_target_pairs={{8,10},{9,11},{24,26},{25,27}} | collective-permute-start | bytes 393224 | tf_op jit(solution)/shard_map/cond/branch_4_fun/ppermute | solution.py:257
  52.5 14.4 %collective-permute-start.142 = (bf16[256,256]{1,0:T(8,128)(2,1)S(1)}, bf16[256,256]{1,0:T(8,128)(2,1)S(1)}, u32[]{:S(2)}, u32[]{:S(2)}) collective-permute-start(bf16[256,256]{1,0:T(8,128)(2,1)S(1)} %get-tuple-element.586), channel_id=1, source_target_pairs={{8,6},{9,7},{24,22},{25,23}} | collective-permute-start | bytes 393224 | tf_op jit(solution)/shard_map/cond/branch_4_fun/ppermute | solution.py:257
  59.1 7.8 %collective-permute-start.144 = (bf16[256,256]{1,0:T(8,128)(2,1)S(1)}, bf16[256,256]{1,0:T(8,128)(2,1)S(1)}, u32[]{:S(2)}, u32[]{:S(2)}) collective-permute-start(bf16[256,256]{1,0:T(8,128)(2,1)S(1)} %add_select_fusion.28), channel_id=1, source_target_pairs={{0,2},{1,3},{16,18},{17,19}} | collective-permute-start | bytes 393224 | tf_op jit(solution)/shard_map/cond/branch_4_fun/ppermute | solution.py:261
  60.4 6.5 %collective-permute-start.143 = (bf16[256,256]{1,0:T(8,128)(2,1)S(1)}, bf16[256,256]{1,0:T(8,128)(2,1)S(1)}, u32[]{:S(2)}, u32[]{:S(2)}) collective-permute-start(bf16[256,256]{1,0:T(8,128)(2,1)S(1)} %add_select_fusion.28), channel_id=1, source_target_pairs={{0,4},{2,6},{8,12},{10,14},{1,5},{3,7},{9,13},{11,15},{16,20},{18,... | collective-permute-start | bytes 393224 | tf_op jit(solution)/shard_map/cond/branch_4_fun/ppermute | solution.py:262
  68.6 6.0 %collective-permute-start.160 = (bf16[2,16,2048]{2,1,0:T(8,128)(2,1)S(1)}, bf16[2,16,2048]{2,1,0:T(8,128)(2,1)S(1)}, u32[]{:S(2)}, u32[]{:S(2)}) collective-permute-start(bf16[2,16,2048]{2,1,0:T(8,128)(2,1)S(1)} %get-tuple-element.658), channel_id=1, source_target_pairs={{0,2},{2,0},{4,6},{6,4},{8,10},{10,8},{12,14},{14,12},{1,3},{3,1},... | collective-permute-start | bytes 393224 | tf_op jit(solution)/shard_map/ppermute | solution.py:323
  68.7 7.2 %collective-permute-start.161 = (bf16[2,16,2048]{2,1,0:T(8,128)(2,1)S(1)}, bf16[2,16,2048]{2,1,0:T(8,128)(2,1)S(1)}, u32[]{:S(2)}, u32[]{:S(2)}) collective-permute-start(bf16[2,16,2048]{2,1,0:T(8,128)(2,1)S(1)} %get-tuple-element.659), channel_id=1, source_target_pairs={{0,4},{2,6},{4,0},{6,2},{8,12},{10,14},{12,8},{14,10},{1,5},{3,7},... | collective-permute-start | bytes 393224 | tf_op jit(solution)/shard_map/ppermute | solution.py:323
  68.7 12.6 %collective-permute-start.162 = (bf16[2,16,2048]{2,1,0:T(8,128)(2,1)S(1)}, bf16[2,16,2048]{2,1,0:T(8,128)(2,1)S(1)}, u32[]{:S(2)}, u32[]{:S(2)}) collective-permute-start(bf16[2,16,2048]{2,1,0:T(8,128)(2,1)S(1)} %get-tuple-element.660), channel_id=1, source_target_pairs={{0,6},{2,4},{4,2},{6,0},{8,14},{10,12},{12,10},{14,8},{1,7},{3,5},... | collective-permute-start | bytes 393224 | tf_op jit(solution)/shard_map/ppermute | solution.py:323
  72.1 15.2 %collective-permute-start.163 = (bf16[2,16,2048]{2,1,0:T(8,128)(2,1)S(1)}, bf16[2,16,2048]{2,1,0:T(8,128)(2,1)S(1)}, u32[]{:S(2)}, u32[]{:S(2)}) collective-permute-start(bf16[2,16,2048]{2,1,0:T(8,128)(2,1)S(1)} %get-tuple-element.661), channel_id=1, source_target_pairs={{0,8},{2,10},{4,12},{6,14},{8,0},{10,2},{12,4},{14,6},{1,9},{3,11}... | collective-permute-start | bytes 393224 | tf_op jit(solution)/shard_map/ppermute | solution.py:323
  72.1 17.8 %collective-permute-start.164 = (bf16[2,16,2048]{2,1,0:T(8,128)(2,1)S(1)}, bf16[2,16,2048]{2,1,0:T(8,128)(2,1)S(1)}, u32[]{:S(2)}, u32[]{:S(2)}) collective-permute-start(bf16[2,16,2048]{2,1,0:T(8,128)(2,1)S(1)} %get-tuple-element.662), channel_id=1, source_target_pairs={{0,10},{2,8},{4,14},{6,12},{8,2},{10,0},{12,6},{14,4},{1,11},{3,9}... | collective-permute-start | bytes 393224 | tf_op jit(solution)/shard_map/ppermute | solution.py:323
  74.6 15.4 %collective-permute-start.165 = (bf16[2,16,2048]{2,1,0:T(8,128)(2,1)S(1)}, bf16[2,16,2048]{2,1,0:T(8,128)(2,1)S(1)}, u32[]{:S(2)}, u32[]{:S(2)}) collective-permute-start(bf16[2,16,2048]{2,1,0:T(8,128)(2,1)S(1)} %get-tuple-element.663), channel_id=1, source_target_pairs={{0,12},{2,14},{4,8},{6,10},{8,4},{10,6},{12,0},{14,2},{1,13},{3,15... | collective-permute-start | bytes 393224 | tf_op jit(solution)/shard_map/ppermute | solution.py:323
  75.9 14.1 %collective-permute-start.166 = (bf16[2,16,2048]{2,1,0:T(8,128)(2,1)S(1)}, bf16[2,16,2048]{2,1,0:T(8,128)(2,1)S(1)}, u32[]{:S(2)}, u32[]{:S(2)}) collective-permute-start(bf16[2,16,2048]{2,1,0:T(8,128)(2,1)S(1)} %get-tuple-element.664), channel_id=1, source_target_pairs={{0,14},{2,12},{4,10},{6,8},{8,6},{10,4},{12,2},{14,0},{1,15},{3,13... | collective-permute-start | bytes 393224 | tf_op jit(solution)/shard_map/ppermute | solution.py:323
  (6 other events, 22.7 us)
